TPU v7x, 128 devices: a whole 4x4x4 slice. The times are simulated.
128 devices in a mesh: rep: 8 (over x, core), tile: 16 (over z, y).
Axes of the slice: x: 4, y: 4, z: 4, core: 2. Of those that a mesh axis runs over, the one named last changes fastest.
Arguments:
- latents: bfloat16 [8, 5, 128, 8, 256], P('rep', None, 'tile'), may hold values from -6 to 6
- cotangent: bfloat16 [8, 5, 128, 8, 256], P('rep', None, 'tile'), may hold values from -0.119628906 to 0.119628906
- kernel_one: bfloat16 [6912, 256], replicated, may hold values from -0.078125 to 0.078125
- kernel_two: bfloat16 [6912, 256], replicated, may hold values from -0.078125 to 0.078125
- error_one: float32 [8, 6912, 256], P('rep', 'tile'), may hold values from -4 to 4
- error_two: float32 [8, 6912, 256], P('rep', 'tile'), may hold values from -4 to 4
- factor_one: float32 [256, 8], replicated, may hold values from -6 to 6
- factor_two: float32 [256, 8], replicated, may hold values from -6 to 6
Outputs:
- approx_one: float32 [6912, 256], P('tile')
- approx_two: float32 [6912, 256], P('tile')
- new_error_one: float32 [8, 6912, 256], P('rep', 'tile')
- new_error_two: float32 [8, 6912, 256], P('rep', 'tile')
- new_factor_one: float32 [256, 8], replicated
- new_factor_two: float32 [256, 8], replicated
All inputs are finite; a program needn't handle non-finite values.
Results may differ from a plain program's by a relative error of at most 0.0075.
Values may be sent and summed in bfloat16 or wider, within the bound.
A program may use at most 320 MiB of HBM per device.

v0:
```python
import jax
import jax.numpy as jnp
from jax import lax
from jax.sharding import PartitionSpec as P

HIGH = lax.Precision.HIGHEST


def padded_2(x, sides, width):
    for axis, dim in sides:
        size, length = (lax.axis_size(axis), x.shape[dim])
        up = [(i, (i + 1) % size) for i in range(size - 1)]
        down = [(j, i) for i, j in up]
        last = lax.slice_in_dim(x, length - width, length, axis=dim)
        leading = lax.slice_in_dim(x, 0, width, axis=dim)
        before = lax.ppermute(last, axis, up)
        after = lax.ppermute(leading, axis, down)
        x = jnp.concatenate([before, x, after], axis=dim)
    return x


def kernel_taps(kernel):
    chans = kernel.shape[1]
    return kernel.reshape(chans, 3, 3, 3, chans).transpose(1, 2, 3, 0, 4)


def add_rim(field):
    return padded_2(field, (("tile", 1),), 1)


def causal_conv(rimmed, kernel):
    result = lax.conv_general_dilated(
        rimmed[None],
        kernel_taps(kernel),
        (1, 1, 1),
        [(2, 0), (0, 0), (1, 1)],
        dimension_numbers=("NDHWC", "DHWIO", "NDHWC"),
        preferred_element_type=jnp.float32,
    )
    return result[0]


def reverse_conv(rimmed, kernel):
    flipped = kernel_taps(kernel)[::-1, ::-1, ::-1].transpose(0, 1, 2, 4, 3)
    result = lax.conv_general_dilated(
        rimmed[None],
        flipped,
        (1, 1, 1),
        [(0, 2), (0, 0), (1, 1)],
        dimension_numbers=("NDHWC", "DHWIO", "NDHWC"),
        preferred_element_type=jnp.float32,
    )
    return result[0]


def silu_slope(value):
    sig = jax.nn.sigmoid(value)
    return sig * (1.0 + value * (1.0 - sig))


def piece_patches(rimmed, first, count):
    part = lax.dynamic_slice_in_dim(rimmed, first, count, 3)
    frames, height, width = (part.shape[0], part.shape[1] - 2, part.shape[2])
    padded = jnp.pad(part, ((2, 0), (0, 0), (1, 1), (0, 0)))
    taps = [
        padded[a : a + frames, b : b + height, e : e + width]
        for a in range(3)
        for b in range(3)
        for e in range(3)
    ]
    stacked = jnp.stack(taps, axis=-1)
    return stacked.reshape(frames * height * width, count * 27)


def shard_gradient(rimmed, slope):
    chans = slope.shape[-1]
    count = chans // lax.axis_size("tile")
    first = lax.axis_index("tile") * count
    empty = jnp.zeros((27 * count, chans), jnp.float32)
    stack_rim = lax.all_gather(rimmed[None], "tile", axis=0, tiled=True)
    stack_slope = lax.all_gather(slope[None], "tile", axis=0, tiled=True)
    patches = jax.vmap(lambda single: piece_patches(single, first, count))(stack_rim)
    patches = patches.reshape(-1, patches.shape[-1])
    flat = stack_slope.reshape(-1, stack_slope.shape[-1])
    return empty + lax.dot_general(
        patches, flat, (((0,), (0,)), ((), ())), preferred_element_type=jnp.float32
    )


def orthonormal(left):
    columns = []
    for j in range(left.shape[2]):
        vector = left[:, :, j]
        if j > 0:
            basis = jnp.stack(columns, axis=2)
            coefs = lax.psum(jnp.einsum("lrk,lr->lk", basis, vector, precision=HIGH), "tile")
            vector = vector - jnp.einsum("lrk,lk->lr", basis, coefs, precision=HIGH)
        length = lax.psum(jnp.sum(vector * vector, axis=1), "tile")
        columns.append(vector / jnp.sqrt(length)[:, None])
    return jnp.stack(columns, axis=2)


def compress(merged, factors):
    replicas = lax.axis_size("rep")
    proj = jnp.einsum("lrc,lck->lrk", merged, factors, precision=HIGH)
    left = lax.psum(proj, "rep") / replicas
    basis = orthonormal(left)
    local_right = jnp.einsum("lrc,lrk->lck", merged, basis, precision=HIGH)
    right = lax.psum(local_right, ("rep", "tile")) / replicas
    approx = jnp.einsum("lrk,lck->lrc", basis, right, precision=HIGH)
    return (approx, merged - approx, right)


def on_device(
    latents, cotangent, kernel_one, kernel_two, error_one, error_two, factor_one, factor_two
):
    rim_input = add_rim(latents[0])
    pre_one = causal_conv(rim_input, kernel_one)
    hidden = jax.nn.silu(pre_one).astype(jnp.bfloat16)
    rim_hidden = add_rim(hidden)
    pre_two = causal_conv(rim_hidden, kernel_two)
    slope_two = (cotangent[0].astype(jnp.float32) * silu_slope(pre_two)).astype(jnp.bfloat16)
    merged_two = shard_gradient(rim_hidden, slope_two) + error_two[0]
    approx_two, fresh_two, right_two = compress(merged_two[None], factor_two[None])
    rim_slope = add_rim(slope_two)
    back_one = reverse_conv(rim_slope, kernel_two)
    slope_one = (back_one * silu_slope(pre_one)).astype(jnp.bfloat16)
    merged_one = shard_gradient(rim_input, slope_one) + error_one[0]
    approx_one, fresh_one, right_one = compress(merged_one[None], factor_one[None])
    return (approx_one[0], approx_two[0], fresh_one, fresh_two, right_one[0], right_two[0])


def solution(mesh):
    placed = (
        P("rep", None, "tile", None, None),
        P("rep", None, "tile", None, None),
        P(),
        P(),
        P("rep", "tile", None),
        P("rep", "tile", None),
        P(),
        P(),
    )
    return jax.shard_map(
        on_device,
        mesh=mesh,
        in_specs=placed,
        out_specs=(
            P("tile", None),
            P("tile", None),
            P("rep", "tile", None),
            P("rep", "tile", None),
            P(),
            P(),
        ),
        check_vma=False,
    )
```

profile of v0, /device:TPU:1, one launch (start us, length us, event | category | flops | bytes accessed | tf_op | source)
XLA Modules:
  0.0 1022.7 jit_solution(10568747914270223441)
XLA Ops:
  8.0 4.0 collective-permute-start
  18.3 8.8 reshape.390
  27.2 8.3 fusion
  40.9 3.7 collective-permute-done.3
  45.7 5.5 reshape.391
  51.2 8.2 fusion.4
  60.5 5.1 collective-permute-start.4
  70.7 9.4 fusion.2
  164.4 5.0 fusion.102
  170.9 50.5 %copy.113 = bf16[16,5,8,8,16,27]{5,4,3,2,1,0:T(8,128)(2,1)} copy(bf16[16,5,8,8,16,27]{4,3,2,1,0,5:T(8,128)(2,1)} %fusion.101) | data formatting | bytes 8847360 | tf_op jit(solution)/shard_map/vmap()/stack | solution.py:71
  221.4 28.4 %reshape.409 = bf16[5120,432]{1,0:T(8,128)(2,1)} reshape(bf16[16,5,8,8,16,27]{5,4,3,2,1,0:T(8,128)(2,1)} %copy.113) | data formatting | bytes 8847360 | tf_op jit(solution)/shard_map/reshape;vmap()/reshape | solution.py:83
  251.3 50.4 %copy.103 = bf16[16,5,8,8,16,27]{5,4,3,2,1,0:T(8,128)(2,1)} copy(bf16[16,5,8,8,16,27]{4,3,2,1,0,5:T(8,128)(2,1)} %fusion.53) | data formatting | bytes 8847360 | tf_op jit(solution)/shard_map/vmap()/stack | solution.py:71
  301.7 28.4 %reshape.389 = bf16[5120,432]{1,0:T(8,128)(2,1)} reshape(bf16[16,5,8,8,16,27]{5,4,3,2,1,0:T(8,128)(2,1)} %copy.103) | data formatting | bytes 8847360 | tf_op jit(solution)/shard_map/reshape;vmap()/reshape | solution.py:83
  330.1 4.9 convolution_add_fusion
  335.6 4.9 convolution_add_fusion.1
  340.9 23.6 %all-reduce.18 = (f32[1,432,8]{1,2,0:T(8,128)S(1)}, f32[1,432,8]{1,2,0:T(8,128)S(1)}) all-reduce(f32[1,432,8]{1,2,0:T(8,128)S(1)} %convolution_bitcast_fusion.1, f32[1,432,8]{1,2,0:T(8,128)S(1)} %convolution_bitcast_fusion), channel_id=1, replica_groups=mesh['rep'=8,'tile'=16] {'rep'}, use_global_device_ids=true, to_apply=%region_0.1 | all-reduce | flops 6912 | bytes 55296 | tf_op jit(solution)/shard_map/psum | solution.py:106
  365.7 31.0 %all-reduce.17 = (f32[1]{0:T(128)}, f32[1]{0:T(128)}) all-reduce(f32[1]{0:T(128)} %bitcast.39, f32[1]{0:T(128)} %bitcast.134), channel_id=1, replica_groups=mesh['rep'=8,'tile'=16] {'tile'}, use_global_device_ids=true, to_apply=%region_2.3 | all-reduce | flops 2 | bytes 16 | tf_op jit(solution)/shard_map/psum | solution.py:98
  399.4 29.3 %all-reduce.16 = (f32[]{:T(128)}, f32[]{:T(128)}) all-reduce(f32[]{:T(128)} %multiply_reduce_fusion.1, f32[]{:T(128)} %multiply_reduce_fusion), channel_id=1, replica_groups=mesh['rep'=8,'tile'=16] {'tile'}, use_global_device_ids=true, to_apply=%region_3.4 | all-reduce | flops 2 | bytes 16 | tf_op jit(solution)/shard_map/psum | solution.py:96
  431.2 30.8 %all-reduce.15 = (f32[1]{0:T(128)}, f32[1]{0:T(128)}) all-reduce(f32[1]{0:T(128)} %bitcast.43, f32[1]{0:T(128)} %bitcast.138), channel_id=1, replica_groups=mesh['rep'=8,'tile'=16] {'tile'}, use_global_device_ids=true, to_apply=%region_5.6 | all-reduce | flops 2 | bytes 16 | tf_op jit(solution)/shard_map/psum | solution.py:98
  465.0 28.5 %all-reduce.14 = (f32[2]{0:T(128)S(1)}, f32[2]{0:T(128)S(1)}) all-reduce(f32[2]{0:T(128)S(1)} %convolution_bitcast_fusion.15, f32[2]{0:T(128)S(1)} %convolution_bitcast_fusion.9), channel_id=1, replica_groups=mesh['rep'=8,'tile'=16] {'tile'}, use_global_device_ids=true, to_apply=%region_6.7 | all-reduce | flops 4 | bytes 32 | tf_op jit(solution)/shard_map/psum | solution.py:96
  495.0 30.6 %all-reduce.13 = (f32[1]{0:T(128)}, f32[1]{0:T(128)}) all-reduce(f32[1]{0:T(128)} %bitcast.52, f32[1]{0:T(128)} %bitcast.147), channel_id=1, replica_groups=mesh['rep'=8,'tile'=16] {'tile'}, use_global_device_ids=true, to_apply=%region_8.9 | all-reduce | flops 2 | bytes 16 | tf_op jit(solution)/shard_map/psum | solution.py:98
  527.3 28.8 %all-reduce.12 = (f32[3]{0:T(128)S(1)}, f32[3]{0:T(128)S(1)}) all-reduce(f32[3]{0:T(128)S(1)} %convolution_bitcast_fusion.14, f32[3]{0:T(128)S(1)} %convolution_bitcast_fusion.8), channel_id=1, replica_groups=mesh['rep'=8,'tile'=16] {'tile'}, use_global_device_ids=true, to_apply=%region_9.10 | all-reduce | flops 6 | bytes 48 | tf_op jit(solution)/shard_map/psum | solution.py:96
  557.6 31.1 %all-reduce.11 = (f32[1]{0:T(128)}, f32[1]{0:T(128)}) all-reduce(f32[1]{0:T(128)} %bitcast.61, f32[1]{0:T(128)} %bitcast.156), channel_id=1, replica_groups=mesh['rep'=8,'tile'=16] {'tile'}, use_global_device_ids=true, to_apply=%region_11.12 | all-reduce | flops 2 | bytes 16 | tf_op jit(solution)/shard_map/psum | solution.py:98
  590.4 28.7 %all-reduce.10 = (f32[4]{0:T(128)S(1)}, f32[4]{0:T(128)S(1)}) all-reduce(f32[4]{0:T(128)S(1)} %convolution_bitcast_fusion.13, f32[4]{0:T(128)S(1)} %convolution_bitcast_fusion.7), channel_id=1, replica_groups=mesh['rep'=8,'tile'=16] {'tile'}, use_global_device_ids=true, to_apply=%region_12.13 | all-reduce | flops 8 | bytes 64 | tf_op jit(solution)/shard_map/psum | solution.py:96
  620.7 31.0 %all-reduce.9 = (f32[1]{0:T(128)}, f32[1]{0:T(128)}) all-reduce(f32[1]{0:T(128)} %bitcast.70, f32[1]{0:T(128)} %bitcast.165), channel_id=1, replica_groups=mesh['rep'=8,'tile'=16] {'tile'}, use_global_device_ids=true, to_apply=%region_14.15 | all-reduce | flops 2 | bytes 16 | tf_op jit(solution)/shard_map/psum | solution.py:98
  653.4 28.5 %all-reduce.8 = (f32[5]{0:T(128)S(1)}, f32[5]{0:T(128)S(1)}) all-reduce(f32[5]{0:T(128)S(1)} %convolution_bitcast_fusion.12, f32[5]{0:T(128)S(1)} %convolution_bitcast_fusion.6), channel_id=1, replica_groups=mesh['rep'=8,'tile'=16] {'tile'}, use_global_device_ids=true, to_apply=%region_15.16 | all-reduce | flops 10 | bytes 80 | tf_op jit(solution)/shard_map/psum | solution.py:96
  683.4 30.6 %all-reduce.7 = (f32[1]{0:T(128)}, f32[1]{0:T(128)}) all-reduce(f32[1]{0:T(128)} %bitcast.79, f32[1]{0:T(128)} %bitcast.174), channel_id=1, replica_groups=mesh['rep'=8,'tile'=16] {'tile'}, use_global_device_ids=true, to_apply=%region_17.18 | all-reduce | flops 2 | bytes 16 | tf_op jit(solution)/shard_map/psum | solution.py:98
  715.8 29.3 %all-reduce.6 = (f32[6]{0:T(128)S(1)}, f32[6]{0:T(128)S(1)}) all-reduce(f32[6]{0:T(128)S(1)} %convolution_bitcast_fusion.11, f32[6]{0:T(128)S(1)} %convolution_bitcast_fusion.5), channel_id=1, replica_groups=mesh['rep'=8,'tile'=16] {'tile'}, use_global_device_ids=true, to_apply=%region_18.19 | all-reduce | flops 12 | bytes 96 | tf_op jit(solution)/shard_map/psum | solution.py:96
  746.5 29.9 %all-reduce.5 = (f32[1]{0:T(128)}, f32[1]{0:T(128)}) all-reduce(f32[1]{0:T(128)} %bitcast.88, f32[1]{0:T(128)} %bitcast.183), channel_id=1, replica_groups=mesh['rep'=8,'tile'=16] {'tile'}, use_global_device_ids=true, to_apply=%region_20.21 | all-reduce | flops 2 | bytes 16 | tf_op jit(solution)/shard_map/psum | solution.py:98
  778.2 29.6 %all-reduce.4 = (f32[7]{0:T(128)S(1)}, f32[7]{0:T(128)S(1)}) all-reduce(f32[7]{0:T(128)S(1)} %convolution_bitcast_fusion.10, f32[7]{0:T(128)S(1)} %convolution_bitcast_fusion.4), channel_id=1, replica_groups=mesh['rep'=8,'tile'=16] {'tile'}, use_global_device_ids=true, to_apply=%region_21.22 | all-reduce | flops 14 | bytes 112 | tf_op jit(solution)/shard_map/psum | solution.py:96
  809.2 30.0 %all-reduce.3 = (f32[1]{0:T(128)}, f32[1]{0:T(128)}) all-reduce(f32[1]{0:T(128)} %bitcast.97, f32[1]{0:T(128)} %bitcast.192), channel_id=1, replica_groups=mesh['rep'=8,'tile'=16] {'tile'}, use_global_device_ids=true, to_apply=%region_23.24 | all-reduce | flops 2 | bytes 16 | tf_op jit(solution)/shard_map/psum | solution.py:98
  841.4 171.3 %all-reduce.2 = (f32[1,256,8]{1,2,0:T(8,128)S(1)}, f32[1,256,8]{1,2,0:T(8,128)S(1)}) all-reduce(f32[1,256,8]{1,2,0:T(8,128)S(1)} %convolution_bitcast_fusion.3, f32[1,256,8]{1,2,0:T(8,128)S(1)} %convolution_bitcast_fusion.2), channel_id=1, replica_groups=mesh['rep'=8,'tile'=16] {'rep','tile'}, use_global_device_ids=true, to_apply=%region_24.25 | all-reduce | flops 4096 | bytes 32768 | tf_op jit(solution)/shard_map/psum | solution.py:109
  (194 shorter events, 128.7 us)
Async XLA Ops:
  7.2 327.9 %copy-start = (f32[256,8]{0,1:T(8,128)S(1)}, f32[256,8]{0,1:T(8,128)}, u32[]{:S(2)}) copy-start(f32[256,8]{0,1:T(8,128)} %param.15) | copy-start | bytes 24580
  7.2 73.8 %all-gather.11.cloned.1.call-start = ((), (), s32[]{:S(2)}) async-start(), calls=%async_computation.2 | async-start | bytes 3481600 | tf_op jit(solution)/shard_map/all_gather | solution.py:80
  8.0 5.3 collective-permute-start
  12.0 4.5 collective-permute-start.1
  18.3 104.4 %all-gather.13.cloned.1.call-start = ((), (), s32[]{:S(2)}) async-start(), calls=%async_computation.3 | async-start | bytes 3481600 | tf_op jit(solution)/shard_map/all_gather | solution.py:80
  27.2 18.5 %copy-start.3 = (bf16[6912,256]{1,0:T(8,128)(2,1)S(1)}, bf16[6912,256]{1,0:T(8,128)(2,1)}, u32[]{:S(2)}) copy-start(bf16[6912,256]{1,0:T(8,128)(2,1)} %param.11) | copy-start | bytes 10616836
  35.5 0.7 copy-start.6
  36.4 4.5 collective-permute-start.2
  39.6 5.0 collective-permute-start.3
  45.4 284.7 %all-gather.9.cloned.1.call-start = ((), (), s32[]{:S(2)}) async-start(), calls=%async_computation.1 | async-start | bytes 2785280 | tf_op jit(solution)/shard_map/all_gather | solution.py:81
  51.2 8.3 copy-start.8
  60.3 275.2 %all-gather.7.cloned.1.call-start = ((), (), s32[]{:S(2)}) async-start(), calls=%async_computation | async-start | bytes 2785280 | tf_op jit(solution)/shard_map/all_gather | solution.py:81
  60.5 7.5 collective-permute-start.4
  65.6 5.1 collective-permute-start.5
  70.7 9.4 copy-start.7
  107.7 4.5 copy-start.1
  149.2 4.4 copy-start.2
  301.7 28.4 %copy-start.9 = (f32[1,432,256]{2,1,0:T(8,128)S(1)}, f32[1,432,256]{2,1,0:T(8,128)}, u32[]{:S(2)}) copy-start(f32[1,432,256]{2,1,0:T(8,128)} %param.13) | copy-start | bytes 1327108
  330.1 5.4 copy-start.10
  335.6 4.9 copy-start.13
  1012.7 3.0 copy-start.11
  1013.3 2.4 copy-start.4
  1014.2 1.5 copy-start.12
  1014.8 0.9 copy-start.5
Sparse Core Ops, SparseCore 0:
  18.4 53.7 all-gather.10
  75.0 46.9 all-gather.12
  124.6 45.0 all-gather.8
  172.3 45.6 all-gather.6
where the time goes:
time: 1030 us; the launch traced here: 1020 us
  blocking collectives  643 us (62%)
  local copies, waits for them, and re-layouts  266 us (26%)
  matrix products  41.8 us (4%)
  between operations  25.9 us (3%)
  other arithmetic  19.8 us (2%)
  starting transfers between devices  16.9 us (2%)
    psum x8, blocking collectives, orthonormal(): length = lax.psum(jnp.sum(vector * vector, axis=1), 'tile')  245 us
    psum x7, blocking collectives, orthonormal(): lax.psum(jnp.einsum('lrk,lr->lk', basis, vector, precision=HIGH), 'tile')  203 us
    psum x1, blocking collectives, compress(): right = lax.psum(local_right, ('rep', 'tile')) / replicas  171 us
    another operation x4, local copies, waits for them, and re-layouts, piece_patches(): stacked = jnp.stack(taps, axis=-1)  104 us
    unnamed x79, local copies, waits for them, and re-layouts  82.9 us
    reshape x2, local copies, waits for them, and re-layouts, shard_gradient(): patches = patches.reshape(-1, patches.shape[-1])  56.8 us
    psum x1, blocking collectives, compress(): left = lax.psum(proj, 'rep') / replicas  23.6 us
  transfers between devices with their start and end apart: 10, of which 3 were waited for; matrix products, arithmetic and copies ran while one was open for 29% of the time, Pallas kernels for 0%

commit v1 on v0

v1 whole, which is shorter than its diff:
```python
import functools

import jax
import jax.numpy as jnp
from jax import lax
from jax.experimental import pallas as pl
from jax.experimental.pallas import tpu as pltpu
from jax.sharding import PartitionSpec as P

MESH = pl.DeviceIdType.MESH
HIGH = lax.Precision.HIGHEST
BF = jnp.bfloat16
F32 = jnp.float32
FR = 5
WC = 8
C = 256
RANK = 8
OWN = 432
NT = (((1,), (1,)), ((), ()))
TN = (((0,), (0,)), ((), ()))


def sigmoid(v):
    return 1.0 / (1.0 + jnp.exp(-v))


def silu_slope(v):
    sig = sigmoid(v)
    return sig * (1.0 + v * (1.0 - sig))


def valid_rows(field, first, tile):
    row = lax.broadcasted_iota(jnp.int32, field.shape, 0) + first
    inside = jnp.logical_and(
        jnp.logical_or(row >= 0, tile > 0), jnp.logical_or(row < 8, tile < 15)
    )
    return jnp.where(inside, field, 0.0)


def spread(field, frame, even, odd):
    rows = field.shape[0]
    col = lax.broadcasted_iota(jnp.int32, field.shape, 1)
    for e in range(3):
        if e == 1:
            moved = field
        else:
            moved = pltpu.roll(field, 1 if e == 0 else WC - 1, 1)
            moved = jnp.where(col == (0 if e == 0 else WC - 1), 0.0, moved)
        even[e, frame, pl.ds(0, rows * WC), :] = moved.reshape(rows * WC, C).astype(BF)
        inner = moved[1 : rows - 1].reshape((rows - 2) * WC, C)
        odd[e, frame, pl.ds(0, (rows - 2) * WC), :] = inner.astype(BF)


def conv(even, odd, rows, weights, total, reverse):
    for a in (2, 1, 0):
        count = 3 + a
        first_in, first_out = (2 - a, 0) if reverse else (0, 2 - a)
        pieces = []
        for b in range(3):
            for e in range(3):
                bb, ee = (2 - b, 2 - e) if reverse else (b, e)
                source = odd if bb == 1 else even
                start = 16 if bb == 2 else 0
                piece = source[ee, pl.ds(first_in, count), pl.ds(start, rows * WC), :]
                pieces.append(piece.reshape(count * rows * WC, C))
        lhs = jnp.concatenate(pieces, axis=1)
        if reverse:
            taps = [weights[a, pl.ds(i * C, C), :] for i in range(9)]
            out = lax.dot_general(
                lhs, jnp.concatenate(taps, axis=1), NT, preferred_element_type=F32
            )
        else:
            out = jnp.dot(lhs, weights[a], preferred_element_type=F32)
        out = out.reshape(count, rows * WC, C)
        if a == 2:
            total[...] = out
        else:
            total[pl.ds(first_out, count)] += out


def turned(field):
    flat = field.reshape(80, C)
    flat = jnp.concatenate([flat, jnp.zeros((48, C), F32)], axis=0)
    return flat.T.astype(BF).reshape(4, 4, 16, 128)


def train_kernel(
    lat, cot, ker_one, ker_two, err_one, err_two, fac_one, fac_two,
    merged, left_out, right_out,
    raw, weights, chunk, lat_ext, cot_ext, even, odd, acc_one, acc_two, acc_three,
    select, turn, turn_in, slopes, patches, part, part_half, part_in, errs,
    proj, right_rep, right_y, right_z, local_sem, send_sem, recv_sem,
):
    tile = lax.axis_index("tile")
    rep = lax.axis_index("rep")
    tz, ty = tile // 4, tile % 4

    def along(axis, d):
        if axis == "z":
            return lax.rem(tz + d, 4) * 4 + ty
        return tz * 4 + lax.rem(ty + d, 4)

    up, down = lax.rem(tile + 15, 16), lax.rem(tile + 1, 16)
    sends = []
    n_send = [0]

    def remote(src, dst, recv, device):
        copy = pltpu.make_async_remote_copy(
            src_ref=src, dst_ref=dst, send_sem=send_sem.at[n_send[0]], recv_sem=recv_sem.at[recv],
            device_id=device, device_id_type=MESH,
        )
        n_send[0] += 1
        copy.start()
        sends.append(copy)

    def arrived(dst, recv):
        pltpu.make_async_remote_copy(
            src_ref=dst, dst_ref=dst, send_sem=send_sem.at[0], recv_sem=recv_sem.at[recv],
            device_id={"tile": up}, device_id_type=MESH,
        ).wait_recv()

    loads = [
        pltpu.make_async_copy(ker_one, raw.at[0], local_sem.at[0]),
        pltpu.make_async_copy(ker_two, raw.at[1], local_sem.at[1]),
        pltpu.make_async_copy(lat, lat_ext.at[:, pl.ds(32, 64)], local_sem.at[2]),
        pltpu.make_async_copy(cot, cot_ext.at[:, pl.ds(16, 64)], local_sem.at[3]),
        pltpu.make_async_copy(err_one, errs.at[0], local_sem.at[4]),
        pltpu.make_async_copy(err_two, errs.at[1], local_sem.at[5]),
    ]
    for load in loads:
        load.start()

    barrier = pltpu.get_barrier_semaphore()
    greeted = [{"tile": up}, {"tile": down}]
    greeted += [{"tile": along("y", d)} for d in range(1, 4)]
    greeted += [{"tile": along("z", d)} for d in range(1, 4)]
    greeted += [{"rep": lax.rem(rep + d, 8)} for d in range(1, 8)]
    for device in greeted:
        pl.semaphore_signal(barrier, inc=1, device_id=device, device_id_type=MESH)
    pl.semaphore_wait(barrier, len(greeted))

    remote(lat.at[:, pl.ds(32, 32)], lat_ext.at[:, pl.ds(0, 32)], 0, {"tile": down})
    remote(lat.at[:, pl.ds(0, 32)], lat_ext.at[:, pl.ds(96, 32)], 1, {"tile": up})
    remote(cot.at[:, pl.ds(48, 16)], cot_ext.at[:, pl.ds(0, 16)], 2, {"tile": down})
    remote(cot.at[:, pl.ds(0, 16)], cot_ext.at[:, pl.ds(80, 16)], 3, {"tile": up})

    held = lax.broadcasted_iota(jnp.int32, (256, 128), 0)
    want = lax.broadcasted_iota(jnp.int32, (256, 128), 1)
    same = (held // 128) == (want // 64)
    held, want = held % 128, want % 64
    for b in range(3):
        for e in range(3):
            hit = jnp.logical_and(held // 8 == want // 8 + b, held % 8 == want % 8 + (e - 1))
            hit = jnp.logical_and(same, hit)
            select[:, pl.ds((b * 3 + e) * 128, 128)] = jnp.where(hit, 1.0, 0.0).astype(BF)

    for k in range(2):
        loads[k].wait()

        def reorder(j, carry, k=k):
            rows = pl.ds(pl.multiple_of(j * OWN, OWN), OWN)
            for half in range(2):
                lanes = pl.ds(half * 128, 128)
                chunk[half] = raw[k, rows, lanes].astype(F32)
                for tap in range(27):
                    picked = chunk[half, pl.ds(tap, 16, stride=27), :].astype(BF)
                    at = pl.multiple_of((tap % 9) * C + j * 16, 16)
                    weights[k, tap // 9, pl.ds(at, 16), lanes] = picked
            return carry

        lax.fori_loop(0, 16, reorder, 0)

    loads[2].wait()
    loads[3].wait()
    arrived(lat_ext.at[:, pl.ds(0, 32)], 0)
    arrived(lat_ext.at[:, pl.ds(96, 32)], 1)

    def enter_one(f, carry):
        field = lat_ext[f].astype(F32).reshape(16, WC, C)[1:15]
        field = valid_rows(field, -3, tile)
        turn[0, f] = turned(field[2:12])
        spread(field, f, even, odd)
        return carry

    lax.fori_loop(0, FR, enter_one, 0)
    own = [
        pltpu.make_async_copy(turn.at[0, :, tz], turn_in.at[0, 0], local_sem.at[6]),
        pltpu.make_async_copy(turn.at[1, :, :, ty], turn_in.at[1, 0], local_sem.at[7]),
    ]
    own[0].start()
    for d in range(1, 4):
        to = lax.rem(tz + d, 4)
        remote(turn.at[0, :, to], turn_in.at[0, d], 4 + d, {"tile": along("z", d)})
    conv(even, odd, 12, weights.at[0], acc_one, False)

    def enter_two(f, carry):
        pre = acc_one[f]
        hidden = (pre * sigmoid(pre)).astype(BF).astype(F32).reshape(12, WC, C)
        hidden = valid_rows(hidden, -2, tile)
        turn[1, f] = turned(hidden[1:11])
        spread(hidden, f, even, odd)
        return carry

    lax.fori_loop(0, FR, enter_two, 0)
    own[1].start()
    for d in range(1, 4):
        to = lax.rem(ty + d, 4)
        remote(turn.at[1, :, :, to], turn_in.at[1, d], 8 + d, {"tile": along("y", d)})
    conv(even, odd, 10, weights.at[1], acc_two, False)

    arrived(cot_ext.at[:, pl.ds(0, 16)], 2)
    arrived(cot_ext.at[:, pl.ds(80, 16)], 3)

    def enter_three(f, carry):
        cots = cot_ext[f].astype(F32)[8:88]
        slope = (cots * silu_slope(acc_two[f])).astype(BF).astype(F32).reshape(10, WC, C)
        slope = valid_rows(slope, -1, tile)
        spread(slope, f, even, odd)
        slopes[1, f, 0] = slope[1:9].reshape(64, C).astype(BF)
        return carry

    lax.fori_loop(0, FR, enter_three, 0)
    for d in range(1, 4):
        remote(slopes.at[1, :, 0], slopes.at[1, :, d], 12 + d, {"tile": along("y", d)})
    conv(even, odd, 8, weights.at[1], acc_three, True)

    def leave(f, carry):
        pre = acc_one[f, pl.ds(16, 64), :]
        slopes[0, f, 0] = (acc_three[f] * silu_slope(pre)).astype(BF)
        return carry

    lax.fori_loop(0, FR, leave, 0)
    for d in range(1, 4):
        remote(slopes.at[0, :, 0], slopes.at[0, :, d], 16 + d, {"tile": along("z", d)})

    for k in range(2):
        own[k].wait()
        for d in range(1, 4):
            arrived(turn_in.at[k, d], 4 + 4 * k + d)
        for p in range(2):
            lhs = jnp.concatenate(
                [turn_in[k, 2 * p + s].reshape(320, 128) for s in range(2)], axis=1
            )
            out = jnp.dot(lhs, select[...], preferred_element_type=F32).astype(BF)
            for f in range(FR):
                for i in range(9):
                    block = out[f * 64 : f * 64 + 64, i * 128 : i * 128 + 128]
                    patches[k, pl.ds(i * 64, 64), pl.ds(f * 256 + p * 128, 128)] = block

    for k in (1, 0):
        for d in range(1, 4):
            arrived(slopes.at[k, :, d], 16 - 4 * k + d)
        for a in range(3):
            count = 3 + a
            rhs = slopes[k, pl.ds(2 - a, count)].reshape(count * 256, C)
            out = jnp.dot(patches[k, :, pl.ds(0, count * 256)], rhs, preferred_element_type=F32)
            out = out.reshape(9, 4, 16, C)
            for j in range(4):
                part[k, j, pl.ds(a * 9, 9)] = out[:, j]
                part_half[k, j, pl.ds(a * 9, 9)] = out[:, j].astype(BF)
        axis, mine = ("z", tz) if k else ("y", ty)
        for d in range(1, 4):
            to = lax.rem(mine + d, 4)
            remote(part_half.at[k, to], part_in.at[k, d], 20 + 4 * k + d, {"tile": along(axis, d)})

    for k in (1, 0):
        mine = tz if k else ty
        loads[4 + k].wait()
        for d in range(1, 4):
            arrived(part_in.at[k, d], 20 + 4 * k + d)
        for tap in range(27):
            grad = part[k, mine, tap]
            for d in range(1, 4):
                grad = grad + part_in[k, d, tap].astype(F32)
            for half in range(2):
                chunk[half, pl.ds(tap, 16, stride=27), :] = grad[:, half * 128 : half * 128 + 128]
        for half in range(2):
            lanes = pl.ds(half * 128, 128)
            merged[k, :, lanes] = chunk[half] + errs[k, :, lanes]
        factor = fac_two if k else fac_one
        proj[rep, pl.ds(k * 8, 8), :] = lax.dot_general(
            factor[...], merged[k], NT, precision=HIGH, preferred_element_type=F32
        )

    for d in range(1, 8):
        remote(proj.at[rep], proj.at[rep], 28 + rep, {"rep": lax.rem(rep + d, 8)})
    for d in range(1, 8):
        source = lax.rem(rep + d, 8)
        arrived(proj.at[source], 28 + source)
    left = proj[0]
    for s in range(1, 8):
        left = left + proj[s]
    left = left * 0.125
    left_out[...] = left

    grams = []
    for k in range(2):
        mine = left[k * 8 : k * 8 + 8]
        right_rep[rep, pl.ds(k * 8, 8), :] = jnp.dot(
            mine, merged[k], precision=HIGH, preferred_element_type=F32
        )
        gram = lax.dot_general(mine, mine, NT, precision=HIGH, preferred_element_type=F32)
        grams.append(jnp.concatenate([gram, jnp.zeros((8, 120), F32)], axis=1))
    for d in range(1, 8):
        remote(right_rep.at[rep], right_rep.at[rep], 36 + rep, {"rep": lax.rem(rep + d, 8)})
    for d in range(1, 8):
        source = lax.rem(rep + d, 8)
        arrived(right_rep.at[source], 36 + source)
    right = right_rep[0]
    for s in range(1, 8):
        right = right + right_rep[s]
    right_y[ty, :, pl.ds(0, 256)] = right
    for k in range(2):
        right_y[ty, pl.ds(k * 8, 8), pl.ds(256, 128)] = grams[k]
    for d in range(1, 4):
        remote(right_y.at[ty], right_y.at[ty], 44 + ty, {"tile": along("y", d)})
    for d in range(1, 4):
        source = lax.rem(ty + d, 4)
        arrived(right_y.at[source], 44 + source)
    right_z[tz] = right_y[0] + right_y[1] + right_y[2] + right_y[3]
    for d in range(1, 4):
        remote(right_z.at[tz], right_z.at[tz], 48 + tz, {"tile": along("z", d)})
    for d in range(1, 4):
        source = lax.rem(tz + d, 4)
        arrived(right_z.at[source], 48 + source)
    right_out[...] = right_z[0] + right_z[1] + right_z[2] + right_z[3]

    for copy in sends:
        copy.wait_send()


def finish_kernel(merged, left, right, approx_one, approx_two, fresh_one, fresh_two, new_one, new_two):
    table = jnp.concatenate([left[...], right[...]], axis=1).reshape(2, RANK, OWN + 384)
    row = lax.broadcasted_iota(jnp.int32, table.shape, 1)
    for j in range(RANK):
        column = OWN + C + j
        pivot = table[:, j : j + 1, column : column + 1]
        scaled = table[:, j : j + 1, :] * lax.rsqrt(pivot)
        coefs = table[:, :, column : column + 1] * lax.rsqrt(pivot)
        table = jnp.where(row == j, scaled, jnp.where(row > j, table - coefs * scaled, table))
    for k, (approx_ref, fresh_ref, new_ref) in enumerate(
        ((approx_one, fresh_one, new_one), (approx_two, fresh_two, new_two))
    ):
        basis = table[k, :, 0:OWN]
        factor = table[k, :, OWN : OWN + C] * 0.125
        approx = lax.dot_general(basis, factor, TN, precision=HIGH, preferred_element_type=F32)
        new_ref[...] = factor
        approx_ref[...] = approx
        fresh_ref[...] = merged[k] - approx


def on_device(
    latents, cotangent, kernel_one, kernel_two, error_one, error_two, factor_one, factor_two
):
    vmem = pl.BlockSpec(memory_space=pltpu.VMEM)
    hbm = pl.BlockSpec(memory_space=pl.ANY)
    sds = jax.ShapeDtypeStruct
    merged, left, right = pl.pallas_call(
        train_kernel,
        out_shape=(sds((2, OWN, C), F32), sds((16, OWN), F32), sds((16, 384), F32)),
        in_specs=[hbm] * 6 + [vmem] * 2,
        out_specs=(vmem,) * 3,
        scratch_shapes=[
            pltpu.VMEM((2, 6912, C), BF),
            pltpu.VMEM((2, 3, 9 * C, C), BF),
            pltpu.VMEM((2, OWN, 128), F32),
            pltpu.VMEM((FR, 128, C), BF),
            pltpu.VMEM((FR, 96, C), BF),
            pltpu.VMEM((3, FR, 112, C), BF),
            pltpu.VMEM((3, FR, 96, C), BF),
            pltpu.VMEM((FR, 96, C), F32),
            pltpu.VMEM((FR, 80, C), F32),
            pltpu.VMEM((FR, 64, C), F32),
            pltpu.VMEM((256, 9 * 128), BF),
            pltpu.VMEM((2, FR, 4, 4, 16, 128), BF),
            pltpu.VMEM((2, 4, FR, 4, 16, 128), BF),
            pltpu.VMEM((2, FR, 4, 64, C), BF),
            pltpu.VMEM((2, 9 * 64, FR * 256), BF),
            pltpu.VMEM((2, 4, 27, 16, C), F32),
            pltpu.VMEM((2, 4, 27, 16, C), BF),
            pltpu.VMEM((2, 4, 27, 16, C), BF),
            pltpu.VMEM((2, OWN, C), F32),
            pltpu.VMEM((8, 16, OWN), F32),
            pltpu.VMEM((8, 16, C), F32),
            pltpu.VMEM((4, 16, 384), F32),
            pltpu.VMEM((4, 16, 384), F32),
            pltpu.SemaphoreType.DMA((8,)),
            pltpu.SemaphoreType.DMA((48,)),
            pltpu.SemaphoreType.DMA((52,)),
        ],
        compiler_params=pltpu.CompilerParams(
            collective_id=0, has_side_effects=True, vmem_limit_bytes=60 * 2**20
        ),
        name="train",
    )(
        latents.reshape(FR, 64, C),
        cotangent.reshape(FR, 64, C),
        kernel_one,
        kernel_two,
        error_one[0],
        error_two[0],
        factor_one.T,
        factor_two.T,
    )
    block, small = sds((OWN, C), F32), sds((RANK, C), F32)
    approx_one, approx_two, fresh_one, fresh_two, new_one, new_two = pl.pallas_call(
        finish_kernel,
        out_shape=(block, block, block, block, small, small),
        in_specs=[vmem] * 3,
        out_specs=(vmem,) * 6,
        compiler_params=pltpu.CompilerParams(vmem_limit_bytes=32 * 2**20),
        name="finish",
    )(merged, left, right)
    return approx_one, approx_two, fresh_one[None], fresh_two[None], new_one.T, new_two.T


def solution(mesh):
    placed = (
        P("rep", None, "tile", None, None),
        P("rep", None, "tile", None, None),
        P(),
        P(),
        P("rep", "tile", None),
        P("rep", "tile", None),
        P(),
        P(),
    )
    return jax.shard_map(
        on_device,
        mesh=mesh,
        in_specs=placed,
        out_specs=(
            P("tile", None),
            P("tile", None),
            P("rep", "tile", None),
            P("rep", "tile", None),
            P(),
            P(),
        ),
        check_vma=False,
    )
```

time: 1030 us -> 69.5 us (0.07)
  blocking collectives: 643 us -> 0 us
  local copies, waits for them, and re-layouts: 266 us -> 2.65 us
  Pallas kernels: 0 us -> 65.1 us
  matrix products: 41.8 us -> 0 us
  between operations: 25.9 us -> 0.65 us
  other arithmetic: 19.8 us -> 0 us
  starting transfers between devices: 16.9 us -> 0 us
    psum x17 -> x0, blocking collectives: 643 us -> none  [the longest x8 245 us: orthonormal(): length = lax.psum(jnp.sum(vector * vector, axis=1), 'tile')]
    another operation x14 -> x0, local copies, waits for them, and re-layouts: 105 us -> none  [the longest x4 104 us: piece_patches(): stacked = jnp.stack(taps, axis=-1)]
    unnamed x79 -> x6, local copies, waits for them, and re-layouts: 82.9 us -> 2.65 us
    reshape x4 -> x0, local copies, waits for them, and re-layouts: 71.2 us -> none  [the longest x2 56.8 us: shard_gradient(): patches = patches.reshape(-1, patches.shape[-1])]
    pallas_call x0 -> x2, Pallas kernels: none -> 65.1 us  [the longest x1 62.3 us: on_device(): pl.pallas_call(train_kernel, out_shape=(sds((2, OWN, C), F32), sds((16, O...]
    conv_general_dilated x3 -> x0, matrix products: 26 us -> none  [the longest x2 16.6 us: causal_conv(): lax.conv_general_dilated(rimmed[None], kernel_taps(kernel), (1, 1, 1), [(...]
    ppermute x6 -> x0, starting transfers between devices: 16.6 us -> none  [the longest x3 12.3 us: padded_2(): before = lax.ppermute(last, axis, up)]
    dot_general x32 -> x0, matrix products: 15.9 us -> none  [the longest x2 9.83 us: shard_gradient(): lax.dot_general(patches, flat, (((0,), (0,)), ((), ())), preferred_elemen...]
  transfers between devices with their start and end apart: 10 -> 0, of which waited for: 3 -> 0; matrix products, arithmetic and copies ran while one was open for 29% -> 0% of each run, Pallas kernels for 0% -> 0%
where the time goes in v1:
time: 69.5 us; the launch traced here: 68.4 us
  Pallas kernels  65.1 us (94%)
  local copies, waits for them, and re-layouts  2.65 us (4%)
    pallas_call x1, Pallas kernels, on_device(): pl.pallas_call(train_kernel, out_shape=(sds((2, OWN, C), F32), sds((16, O...  62.3 us
    pallas_call x1, Pallas kernels, on_device(): pl.pallas_call(finish_kernel, out_shape=(block, block, block, block, smal...  2.82 us
    unnamed x6, local copies, waits for them, and re-layouts  2.65 us

profile of v1, /device:TPU:1, one launch (start us, length us, event | category | flops | bytes accessed | tf_op | source)
XLA Modules:
  0.0 68.4 jit_solution(15827205161798420827)
XLA Ops:
  0.6 62.3 %train.1 = (f32[2,432,256]{2,1,0:T(8,128)}, f32[16,432]{1,0:T(8,128)}, f32[16,384]{1,0:T(8,128)}) custom-call(bf16[5,64,256]{2,1,0:T(8,128)(2,1)} %bitcast.12, bf16[5,64,256]{2,1,0:T(8,128)(2,1)} %bitcast.13, bf16[6912,256]{1,0:T(8,128)(2,1)} %ker_one.1, bf16[6912,256]{1,0:T(8,128)(2,1)} %ker_two.1, f32[432,256]{1,0:T(8,128)} %bitcast.10, ...), custom_call_target="tpu_custom_call" | custom-call | tf_op jit(solution)/shard_map/train/pallas_call | solution.py:358
  62.9 0.0 copy-start
  62.9 1.2 %copy-done = f32[2,432,256]{2,1,0:T(8,128)S(1)} copy-done((f32[2,432,256]{2,1,0:T(8,128)S(1)}, f32[2,432,256]{2,1,0:T(8,128)}, u32[]{:S(2)}) %copy-start) | copy-done | bytes 884760
  64.1 0.0 copy-start.1
  64.1 0.8 %copy-done.1 = f32[16,432]{1,0:T(8,128)S(1)} copy-done((f32[16,432]{1,0:T(8,128)S(1)}, f32[16,432]{1,0:T(8,128)}, u32[]{:S(2)}) %copy-start.1) | copy-done | bytes 27672
  64.9 0.0 copy-start.2
  64.9 0.7 %copy-done.2 = f32[16,384]{1,0:T(8,128)S(1)} copy-done((f32[16,384]{1,0:T(8,128)S(1)}, f32[16,384]{1,0:T(8,128)}, u32[]{:S(2)}) %copy-start.2) | copy-done | bytes 24600
  65.6 2.8 %finish.1 = (f32[432,256]{1,0:T(8,128)}, f32[432,256]{1,0:T(8,128)}, f32[432,256]{1,0:T(8,128)}, f32[432,256]{1,0:T(8,128)}, f32[8,256]{1,0:T(8,128)}, /*index=5*/f32[8,256]{1,0:T(8,128)}) custom-call(f32[2,432,256]{2,1,0:T(8,128)S(1)} %copy-done, f32[16,432]{1,0:T(8,128)S(1)} %copy-done.1, f32[16,384]{1,0:T(8,128)S(1)} %copy-done.2), custom_call_target="tpu_custom_call" | custom-call | tf_op jit(solution)/shard_map/finish/pallas_call | solution.py:406
Async XLA Ops:
  62.9 1.2 %copy-start = (f32[2,432,256]{2,1,0:T(8,128)S(1)}, f32[2,432,256]{2,1,0:T(8,128)}, u32[]{:S(2)}) copy-start(f32[2,432,256]{2,1,0:T(8,128)} %get-tuple-element.15.merged) | copy-start | bytes 2654212
  64.1 0.8 %copy-start.1 = (f32[16,432]{1,0:T(8,128)S(1)}, f32[16,432]{1,0:T(8,128)}, u32[]{:S(2)}) copy-start(f32[16,432]{1,0:T(8,128)} %get-tuple-element.16.left) | copy-start | bytes 82948
  64.9 0.7 %copy-start.2 = (f32[16,384]{1,0:T(8,128)S(1)}, f32[16,384]{1,0:T(8,128)}, u32[]{:S(2)}) copy-start(f32[16,384]{1,0:T(8,128)} %get-tuple-element.17.right) | copy-start | bytes 73732

commit v2 on v1

--- a/solution.py
+++ b/solution.py
@@ -84,16 +84,42 @@
     return flat.T.astype(BF).reshape(4, 4, 16, 128)
 
 
+def split(v):
+    high = v.astype(BF)
+    rest = v - high.astype(F32)
+    mid = rest.astype(BF)
+    low = (rest - mid.astype(F32)).astype(BF)
+    return jnp.concatenate([high.astype(F32), mid.astype(F32), low.astype(F32)], axis=0).astype(BF)
+
+
 def train_kernel(
     lat, cot, ker_one, ker_two, err_one, err_two, fac_one, fac_two,
-    merged, left_out, right_out,
+    merged, table,
     raw, weights, chunk, lat_ext, cot_ext, even, odd, acc_one, acc_two, acc_three,
-    select, turn, turn_in, slopes, patches, part, part_half, part_in, errs,
-    proj, right_rep, right_y, right_z, local_sem, send_sem, recv_sem,
+    select, order, turn, turn_in, slopes, patches, part, part_half, part_rest, part_in, errs, err_rows,
+    err_proj, thin, proj, proj_in, left_in, lefts, right, grams, right_pair, right_in, right_far, right_all, whole_rows,
+    local_sem, send_sem, recv_sem,
 ):
     tile = lax.axis_index("tile")
     rep = lax.axis_index("rep")
     tz, ty = tile // 4, tile % 4
+    rx, core = rep // 2, rep % 2
+    near = core * tz + (1 - core) * ty
+    other = core * ty + (1 - core) * tz
+    here = rx * 4 + near
+    pair = {"rep": rx * 2 + 1 - core}
+    group = [(dx, dg) for dx in range(4) for dg in range(4) if dx or dg]
+
+    def place(dx, dg):
+        return lax.rem(rx + dx, 4) * 4 + lax.rem(near + dg, 4)
+
+    def member(dx, dg):
+        z, y = lax.rem(tz + core * dg, 4), lax.rem(ty + (1 - core) * dg, 4)
+        return {"rep": lax.rem(rx + dx, 4) * 2 + core, "tile": z * 4 + y}
+
+    def across(d):
+        z, y = lax.rem(tz + (1 - core) * d, 4), lax.rem(ty + core * d, 4)
+        return {"tile": z * 4 + y}
 
     def along(axis, d):
         if axis == "z":
@@ -101,6 +127,8 @@
         return tz * 4 + lax.rem(ty + d, 4)
 
     up, down = lax.rem(tile + 15, 16), lax.rem(tile + 1, 16)
+
+    region = pl.when(tile >= 0)
     sends = []
     n_send = [0]
 
@@ -119,14 +147,57 @@
             device_id={"tile": up}, device_id_type=MESH,
         ).wait_recv()
 
+    def send_block(k, d):
+        to = {"tile": along("y" if k else "z", d)}
+        remote(slopes.at[k, :, 0], slopes.at[k, :, d], 16 - 4 * k + d, to)
+
+    def send_part(k, a, d):
+        to = {"tile": along("z" if k else "y", d)}
+        target = lax.rem((tz if k else ty) + d, 4)
+        remote(part_half.at[k, a, target], part_in.at[k, d, a], 92 + 9 * k + 3 * a + d - 1, to)
+
+    def send_slopes(k):
+        factor = split((fac_two if k else fac_one)[...])
+        rows = slopes[k, :, 0].reshape(320, C)
+        out = lax.dot_general(factor, rows, NT, preferred_element_type=F32)
+        thin[k, 0] = out[0:8] + out[8:16] + out[16:24]
+        axis = "y" if k else "z"
+        for d in range(1, 4):
+            remote(thin.at[k, 0], thin.at[k, d], 28 + 4 * k + d, {"tile": along(axis, d)})
+        for d in (1, 3, 2) if k else (1, 3):
+            send_block(k, d)
+
+    def gradients(k):
+        for d in range(1, 4):
+            arrived(slopes.at[k, :, d], 16 - 4 * k + d)
+        mine = tz if k else ty
+
+        @region
+        def _():
+            for a in range(3):
+                count = 3 + a
+                rhs = slopes[k, pl.ds(2 - a, count)].reshape(count * 256, C)
+                out = jnp.dot(patches[k, :, pl.ds(0, count * 256)], rhs, preferred_element_type=F32)
+                part[k, a] = out.reshape(4, 144, C)
+                part[k, a, mine] += err_rows[k, a]
+            for a in range(3):
+                out = part[k, a]
+                half = out.astype(BF)
+                part_half[k, a] = half
+                part_rest[k, a] = (out - half.astype(F32)).astype(BF)
+
     loads = [
         pltpu.make_async_copy(ker_one, raw.at[0], local_sem.at[0]),
         pltpu.make_async_copy(ker_two, raw.at[1], local_sem.at[1]),
         pltpu.make_async_copy(lat, lat_ext.at[:, pl.ds(32, 64)], local_sem.at[2]),
         pltpu.make_async_copy(cot, cot_ext.at[:, pl.ds(16, 64)], local_sem.at[3]),
-        pltpu.make_async_copy(err_one, errs.at[0], local_sem.at[4]),
-        pltpu.make_async_copy(err_two, errs.at[1], local_sem.at[5]),
     ]
+    for k, err in enumerate((err_one, err_two)):
+        for half in range(2):
+            lanes = pl.ds(half * 128, 128)
+            loads.append(
+                pltpu.make_async_copy(err.at[:, lanes], errs.at[k, half], local_sem.at[8 + 2 * k + half])
+            )
     for load in loads:
         load.start()
 
@@ -134,7 +205,7 @@
     greeted = [{"tile": up}, {"tile": down}]
     greeted += [{"tile": along("y", d)} for d in range(1, 4)]
     greeted += [{"tile": along("z", d)} for d in range(1, 4)]
-    greeted += [{"rep": lax.rem(rep + d, 8)} for d in range(1, 8)]
+    greeted += [pair] + [member(dx, dg) for dx, dg in group if dx]
     for device in greeted:
         pl.semaphore_signal(barrier, inc=1, device_id=device, device_id_type=MESH)
     pl.semaphore_wait(barrier, len(greeted))
@@ -153,6 +224,10 @@
             hit = jnp.logical_and(held // 8 == want // 8 + b, held % 8 == want % 8 + (e - 1))
             hit = jnp.logical_and(same, hit)
             select[:, pl.ds((b * 3 + e) * 128, 128)] = jnp.where(hit, 1.0, 0.0).astype(BF)
+
+    source = lax.broadcasted_iota(jnp.int32, (OWN, OWN), 0)
+    target = lax.broadcasted_iota(jnp.int32, (OWN, OWN), 1)
+    order[...] = jnp.where(target == (source % 16) * 27 + source // 16, 1.0, 0.0).astype(BF)
 
     for k in range(2):
         loads[k].wait()
@@ -170,6 +245,33 @@
 
         lax.fori_loop(0, 16, reorder, 0)
 
+    for k in range(2):
+        mine = tz if k else ty
+        for half in range(2):
+            loads[4 + 2 * k + half].wait()
+
+        @region
+        def _(k=k, mine=mine):
+            for half in range(2):
+                for tap in range(27):
+                    rows = errs[k, half, pl.ds(tap, 16, stride=27), :]
+                    err_rows[k, tap // 9, pl.ds((tap % 9) * 16, 16), pl.ds(half * 128, 128)] = rows
+            out = err_rows[k].reshape(OWN, C)
+            high = out.astype(BF)
+            rest = (out - high.astype(F32)).astype(BF)
+            factor = split((fac_two if k else fac_one)[...])
+            out = lax.dot_general(factor, high, NT, preferred_element_type=F32)
+            out += lax.dot_general(factor, rest, NT, preferred_element_type=F32)
+            out = out[0:8] + out[8:16] + out[16:24]
+            err_proj[k] = jnp.concatenate(
+                [
+                    jnp.where(mine == j, out[:, a * 144 : a * 144 + 144], 0.0)
+                    for a in range(3)
+                    for j in range(4)
+                ],
+                axis=1,
+            )
+
     loads[2].wait()
     loads[3].wait()
     arrived(lat_ext.at[:, pl.ds(0, 32)], 0)
@@ -191,7 +293,7 @@
     for d in range(1, 4):
         to = lax.rem(tz + d, 4)
         remote(turn.at[0, :, to], turn_in.at[0, d], 4 + d, {"tile": along("z", d)})
-    conv(even, odd, 12, weights.at[0], acc_one, False)
+    region(lambda: conv(even, odd, 12, weights.at[0], acc_one, False))
 
     def enter_two(f, carry):
         pre = acc_one[f]
@@ -206,7 +308,7 @@
     for d in range(1, 4):
         to = lax.rem(ty + d, 4)
         remote(turn.at[1, :, :, to], turn_in.at[1, d], 8 + d, {"tile": along("y", d)})
-    conv(even, odd, 10, weights.at[1], acc_two, False)
+    region(lambda: conv(even, odd, 10, weights.at[1], acc_two, False))
 
     arrived(cot_ext.at[:, pl.ds(0, 16)], 2)
     arrived(cot_ext.at[:, pl.ds(80, 16)], 3)
@@ -220,9 +322,8 @@
         return carry
 
     lax.fori_loop(0, FR, enter_three, 0)
-    for d in range(1, 4):
-        remote(slopes.at[1, :, 0], slopes.at[1, :, d], 12 + d, {"tile": along("y", d)})
-    conv(even, odd, 8, weights.at[1], acc_three, True)
+    send_slopes(1)
+    region(lambda: conv(even, odd, 8, weights.at[1], acc_three, True))
 
     def leave(f, carry):
         pre = acc_one[f, pl.ds(16, 64), :]
@@ -230,123 +331,206 @@
         return carry
 
     lax.fori_loop(0, FR, leave, 0)
-    for d in range(1, 4):
-        remote(slopes.at[0, :, 0], slopes.at[0, :, d], 16 + d, {"tile": along("z", d)})
+    send_slopes(0)
 
     for k in range(2):
         own[k].wait()
         for d in range(1, 4):
             arrived(turn_in.at[k, d], 4 + 4 * k + d)
-        for p in range(2):
-            lhs = jnp.concatenate(
-                [turn_in[k, 2 * p + s].reshape(320, 128) for s in range(2)], axis=1
-            )
-            out = jnp.dot(lhs, select[...], preferred_element_type=F32).astype(BF)
-            for f in range(FR):
-                for i in range(9):
-                    block = out[f * 64 : f * 64 + 64, i * 128 : i * 128 + 128]
-                    patches[k, pl.ds(i * 64, 64), pl.ds(f * 256 + p * 128, 128)] = block
+
+        @region
+        def _(k=k):
+            for p in range(2):
+                lhs = jnp.concatenate(
+                    [turn_in[k, 2 * p + s].reshape(320, 128) for s in range(2)], axis=1
+                )
+                out = jnp.dot(lhs, select[...], preferred_element_type=F32).astype(BF)
+                for f in range(FR):
+                    for i in range(9):
+                        for j in range(4):
+                            block = out[f * 64 + j * 16 : f * 64 + j * 16 + 16, i * 128 : i * 128 + 128]
+                            rows = pl.ds(j * 144 + i * 16, 16)
+                            patches[k, rows, pl.ds(f * 256 + p * 128, 128)] = block
 
     for k in (1, 0):
         for d in range(1, 4):
-            arrived(slopes.at[k, :, d], 16 - 4 * k + d)
-        for a in range(3):
-            count = 3 + a
-            rhs = slopes[k, pl.ds(2 - a, count)].reshape(count * 256, C)
-            out = jnp.dot(patches[k, :, pl.ds(0, count * 256)], rhs, preferred_element_type=F32)
-            out = out.reshape(9, 4, 16, C)
-            for j in range(4):
-                part[k, j, pl.ds(a * 9, 9)] = out[:, j]
-                part_half[k, j, pl.ds(a * 9, 9)] = out[:, j].astype(BF)
-        axis, mine = ("z", tz) if k else ("y", ty)
-        for d in range(1, 4):
-            to = lax.rem(mine + d, 4)
-            remote(part_half.at[k, to], part_in.at[k, d], 20 + 4 * k + d, {"tile": along(axis, d)})
-
+            arrived(thin.at[k, d], 28 + 4 * k + d)
+
+        @region
+        def _(k=k):
+            blocks = [thin[k, d] for d in range(4)]
+            wide = jnp.concatenate(
+                [blocks[d][:, f * 64 : f * 64 + 64] for f in range(FR) for d in range(4)], axis=1
+            )
+            wide = split(wide)
+            outs = []
+            for a in range(3):
+                count = 3 + a
+                out = lax.dot_general(
+                    wide[:, (2 - a) * 256 :], patches[k, :, pl.ds(0, count * 256)], NT,
+                    preferred_element_type=F32,
+                )
+                outs.append(out[0:8] + out[8:16] + out[16:24])
+            sample = jnp.concatenate(outs, axis=1) + err_proj[k]
+            sample = jnp.concatenate([sample, jnp.zeros((8, 2048 - 1728), F32)], axis=1)
+            for q in range(16):
+                proj[k, q] = sample[:, q * 128 : q * 128 + 128]
+
+    remote(proj.at[1 - core], proj_in, 36, pair)
+    arrived(proj_in, 36)
+    for q in range(16):
+        proj_in[q] = proj_in[q] + proj[core, q]
+    for dx, dg in group:
+        to = place(dx, dg)
+        remote(proj_in.at[to], left_in.at[here], 37 + here, member(dx, dg))
+    left_in[here] = proj_in[here]
+    send_block(0, 2)
+
+    gradients(1)
+    for dx, dg in group:
+        source = place(dx, dg)
+        arrived(left_in.at[source], 37 + source)
+    piece = left_in[0]
+    for q in range(1, 16):
+        piece = piece + left_in[q]
+    lefts[core, here] = piece * 0.125
+    for dx, dg in group:
+        remote(lefts.at[core, here], lefts.at[core, here], 53 + here, member(dx, dg))
+    for a in range(3):
+        for d in (1, 3):
+            send_part(1, a, d)
+    gradients(0)
+    for d in (1, 3):
+        send_part(0, 2, d)
+    for dx, dg in group:
+        source = place(dx, dg)
+        arrived(lefts.at[core, source], 53 + source)
+    remote(lefts.at[core], lefts.at[core], 69, pair)
+    arrived(lefts.at[1 - core], 69)
+
+    for k in range(2):
+
+        @region
+        def _(k=k):
+            whole = jnp.concatenate([lefts[k, q] for q in range(16)], axis=1)[:, 0:1728]
+            pieces = split(whole)
+            out = jnp.dot(pieces, part_half[k].reshape(1728, C), preferred_element_type=F32)
+            out += jnp.dot(pieces, part_rest[k].reshape(1728, C), preferred_element_type=F32)
+            right[k] = out[0:8] + out[8:16] + out[16:24]
+
+    remote(right.at[1 - core], right_pair, 70, pair)
+    arrived(right_pair, 70)
+    right_in[here] = right_pair[...] + right[core]
+    for dx, dg in group:
+        remote(right_in.at[here], right_in.at[here], 71 + here, member(dx, dg))
+    for a in range(2):
+        for d in (1, 3):
+            send_part(0, a, d)
+        send_part(1, a, 2)
+
+    for k in range(2):
+        mine = tz if k else ty
+
+        @region
+        def _(k=k, mine=mine):
+            whole = jnp.concatenate([lefts[k, q] for q in range(16)], axis=1)[:, 0:1728]
+            gram = lax.dot_general(whole, whole, NT, precision=HIGH, preferred_element_type=F32)
+            grams[k] = jnp.concatenate([gram, jnp.zeros((8, 120), F32)], axis=1)
+            rows = []
+            for a in range(3):
+                found = jnp.zeros((8, 144), F32)
+                for j in range(4):
+                    at = a * 576 + j * 144
+                    found = jnp.where(mine == j, whole[:, at : at + 144], found)
+                rows.append(found)
+            out = split(jnp.concatenate(rows, axis=1))
+            out = jnp.dot(out, order[...], preferred_element_type=F32)
+            table[k, :, pl.ds(0, OWN)] = out[0:8] + out[8:16] + out[16:24]
+
+    for dx, dg in group:
+        source = place(dx, dg)
+        arrived(right_in.at[source], 71 + source)
+    total = right_in[0]
+    for q in range(1, 16):
+        total = total + right_in[q]
+    right_far[other, :, pl.ds(0, 256)] = total
+    right_far[other, :, pl.ds(256, 128)] = grams[core]
+    for d in range(1, 4):
+        remote(right_far.at[other], right_far.at[other], 87 + other, across(d))
+    send_part(1, 2, 2)
+    for a in range(3):
+        send_part(0, a, 2)
+
+    for d in range(1, 4):
+        source = lax.rem(other + d, 4)
+        arrived(right_far.at[source], 87 + source)
+    right_all[core] = right_far[0] + right_far[1] + right_far[2] + right_far[3]
+    remote(right_all.at[core], right_all.at[core], 91, pair)
+    arrived(right_all.at[1 - core], 91)
+    table[:, :, pl.ds(512, 384)] = right_all[...]
+
+    stores = []
     for k in (1, 0):
         mine = tz if k else ty
-        loads[4 + k].wait()
-        for d in range(1, 4):
-            arrived(part_in.at[k, d], 20 + 4 * k + d)
-        for tap in range(27):
-            grad = part[k, mine, tap]
+        for a in range(3):
             for d in range(1, 4):
-                grad = grad + part_in[k, d, tap].astype(F32)
+                arrived(part_in.at[k, d, a], 92 + 9 * k + 3 * a + d - 1)
+
+        @region
+        def _(k=k, mine=mine):
+            for tap in range(27):
+                a, rows = tap // 9, pl.ds((tap % 9) * 16, 16)
+                grad = part[k, a, mine, rows, :]
+                for d in range(1, 4):
+                    grad = grad + part_in[k, d, a, rows, :].astype(F32)
+                for half in range(2):
+                    chunk[half, pl.ds(tap, 16, stride=27), :] = grad[:, half * 128 : half * 128 + 128]
             for half in range(2):
-                chunk[half, pl.ds(tap, 16, stride=27), :] = grad[:, half * 128 : half * 128 + 128]
-        for half in range(2):
-            lanes = pl.ds(half * 128, 128)
-            merged[k, :, lanes] = chunk[half] + errs[k, :, lanes]
-        factor = fac_two if k else fac_one
-        proj[rep, pl.ds(k * 8, 8), :] = lax.dot_general(
-            factor[...], merged[k], NT, precision=HIGH, preferred_element_type=F32
-        )
-
-    for d in range(1, 8):
-        remote(proj.at[rep], proj.at[rep], 28 + rep, {"rep": lax.rem(rep + d, 8)})
-    for d in range(1, 8):
-        source = lax.rem(rep + d, 8)
-        arrived(proj.at[source], 28 + source)
-    left = proj[0]
-    for s in range(1, 8):
-        left = left + proj[s]
-    left = left * 0.125
-    left_out[...] = left
-
-    grams = []
-    for k in range(2):
-        mine = left[k * 8 : k * 8 + 8]
-        right_rep[rep, pl.ds(k * 8, 8), :] = jnp.dot(
-            mine, merged[k], precision=HIGH, preferred_element_type=F32
-        )
-        gram = lax.dot_general(mine, mine, NT, precision=HIGH, preferred_element_type=F32)
-        grams.append(jnp.concatenate([gram, jnp.zeros((8, 120), F32)], axis=1))
-    for d in range(1, 8):
-        remote(right_rep.at[rep], right_rep.at[rep], 36 + rep, {"rep": lax.rem(rep + d, 8)})
-    for d in range(1, 8):
-        source = lax.rem(rep + d, 8)
-        arrived(right_rep.at[source], 36 + source)
-    right = right_rep[0]
-    for s in range(1, 8):
-        right = right + right_rep[s]
-    right_y[ty, :, pl.ds(0, 256)] = right
-    for k in range(2):
-        right_y[ty, pl.ds(k * 8, 8), pl.ds(256, 128)] = grams[k]
-    for d in range(1, 4):
-        remote(right_y.at[ty], right_y.at[ty], 44 + ty, {"tile": along("y", d)})
-    for d in range(1, 4):
-        source = lax.rem(ty + d, 4)
-        arrived(right_y.at[source], 44 + source)
-    right_z[tz] = right_y[0] + right_y[1] + right_y[2] + right_y[3]
-    for d in range(1, 4):
-        remote(right_z.at[tz], right_z.at[tz], 48 + tz, {"tile": along("z", d)})
-    for d in range(1, 4):
-        source = lax.rem(tz + d, 4)
-        arrived(right_z.at[source], 48 + source)
-    right_out[...] = right_z[0] + right_z[1] + right_z[2] + right_z[3]
-
+                whole_rows[k, :, pl.ds(half * 128, 128)] = chunk[half]
+
+        stores.append(pltpu.make_async_copy(whole_rows.at[k], merged.at[k], local_sem.at[k]))
+        stores[-1].start()
+    for store in stores:
+        store.wait()
     for copy in sends:
         copy.wait_send()
 
 
-def finish_kernel(merged, left, right, approx_one, approx_two, fresh_one, fresh_two, new_one, new_two):
-    table = jnp.concatenate([left[...], right[...]], axis=1).reshape(2, RANK, OWN + 384)
+def finish_kernel(
+    merged, table_in, approx_one, approx_two, fresh_one, fresh_two, new_one, new_two,
+    table_ref, rows, approx_ref, fresh_ref, sem,
+):
+    load = pltpu.make_async_copy(table_in, table_ref, sem.at[0])
+    load.start()
+    loads = [pltpu.make_async_copy(merged.at[k], rows.at[k], sem.at[1 + k]) for k in range(2)]
+    for copy in loads:
+        copy.start()
+    load.wait()
+    table = table_ref[...]
     row = lax.broadcasted_iota(jnp.int32, table.shape, 1)
     for j in range(RANK):
-        column = OWN + C + j
-        pivot = table[:, j : j + 1, column : column + 1]
-        scaled = table[:, j : j + 1, :] * lax.rsqrt(pivot)
-        coefs = table[:, :, column : column + 1] * lax.rsqrt(pivot)
+        column = 512 + C + j
+        scale = lax.rsqrt(table[:, j : j + 1, column : column + 1])
+        scaled = table[:, j : j + 1, :] * scale
+        coefs = table[:, :, column : column + 1] * scale
         table = jnp.where(row == j, scaled, jnp.where(row > j, table - coefs * scaled, table))
-    for k, (approx_ref, fresh_ref, new_ref) in enumerate(
+    stores = []
+    for k, (approx_out, fresh_out, new_ref) in enumerate(
         ((approx_one, fresh_one, new_one), (approx_two, fresh_two, new_two))
     ):
         basis = table[k, :, 0:OWN]
-        factor = table[k, :, OWN : OWN + C] * 0.125
+        factor = table[k, :, 512 : 512 + C] * 0.125
         approx = lax.dot_general(basis, factor, TN, precision=HIGH, preferred_element_type=F32)
         new_ref[...] = factor
-        approx_ref[...] = approx
-        fresh_ref[...] = merged[k] - approx
+        approx_ref[k] = approx
+        stores.append(pltpu.make_async_copy(approx_ref.at[k], approx_out, sem.at[3 + k]))
+        stores[-1].start()
+        loads[k].wait()
+        fresh_ref[k] = rows[k] - approx
+        stores.append(pltpu.make_async_copy(fresh_ref.at[k], fresh_out, sem.at[5 + k]))
+        stores[-1].start()
+    for copy in stores:
+        copy.wait()
 
 
 def on_device(
@@ -355,11 +539,11 @@
     vmem = pl.BlockSpec(memory_space=pltpu.VMEM)
     hbm = pl.BlockSpec(memory_space=pl.ANY)
     sds = jax.ShapeDtypeStruct
-    merged, left, right = pl.pallas_call(
+    merged, table = pl.pallas_call(
         train_kernel,
-        out_shape=(sds((2, OWN, C), F32), sds((16, OWN), F32), sds((16, 384), F32)),
+        out_shape=(sds((2, OWN, C), F32), sds((2, RANK, 896), F32)),
         in_specs=[hbm] * 6 + [vmem] * 2,
-        out_specs=(vmem,) * 3,
+        out_specs=(hbm, vmem),
         scratch_shapes=[
             pltpu.VMEM((2, 6912, C), BF),
             pltpu.VMEM((2, 3, 9 * C, C), BF),
@@ -372,21 +556,33 @@
             pltpu.VMEM((FR, 80, C), F32),
             pltpu.VMEM((FR, 64, C), F32),
             pltpu.VMEM((256, 9 * 128), BF),
+            pltpu.VMEM((OWN, OWN), BF),
             pltpu.VMEM((2, FR, 4, 4, 16, 128), BF),
             pltpu.VMEM((2, 4, FR, 4, 16, 128), BF),
             pltpu.VMEM((2, FR, 4, 64, C), BF),
             pltpu.VMEM((2, 9 * 64, FR * 256), BF),
-            pltpu.VMEM((2, 4, 27, 16, C), F32),
-            pltpu.VMEM((2, 4, 27, 16, C), BF),
-            pltpu.VMEM((2, 4, 27, 16, C), BF),
+            pltpu.VMEM((2, 3, 4, 144, C), F32),
+            pltpu.VMEM((2, 3, 4, 144, C), BF),
+            pltpu.VMEM((2, 3, 4, 144, C), BF),
+            pltpu.VMEM((2, 4, 3, 144, C), BF),
+            pltpu.VMEM((2, 2, OWN, 128), F32),
+            pltpu.VMEM((2, 3, 144, C), F32),
+            pltpu.VMEM((2, 8, 1728), F32),
+            pltpu.VMEM((2, 4, 8, 320), F32),
+            pltpu.VMEM((2, 16, 8, 128), F32),
+            pltpu.VMEM((16, 8, 128), F32),
+            pltpu.VMEM((16, 8, 128), F32),
+            pltpu.VMEM((2, 16, 8, 128), F32),
+            pltpu.VMEM((2, 8, C), F32),
+            pltpu.VMEM((2, 8, 128), F32),
+            pltpu.VMEM((8, C), F32),
+            pltpu.VMEM((16, 8, C), F32),
+            pltpu.VMEM((4, 8, 384), F32),
+            pltpu.VMEM((2, 8, 384), F32),
             pltpu.VMEM((2, OWN, C), F32),
-            pltpu.VMEM((8, 16, OWN), F32),
-            pltpu.VMEM((8, 16, C), F32),
-            pltpu.VMEM((4, 16, 384), F32),
-            pltpu.VMEM((4, 16, 384), F32),
-            pltpu.SemaphoreType.DMA((8,)),
-            pltpu.SemaphoreType.DMA((48,)),
-            pltpu.SemaphoreType.DMA((52,)),
+            pltpu.SemaphoreType.DMA((12,)),
+            pltpu.SemaphoreType.DMA((96,)),
+            pltpu.SemaphoreType.DMA((110,)),
         ],
         compiler_params=pltpu.CompilerParams(
             collective_id=0, has_side_effects=True, vmem_limit_bytes=60 * 2**20
@@ -406,11 +602,18 @@
     approx_one, approx_two, fresh_one, fresh_two, new_one, new_two = pl.pallas_call(
         finish_kernel,
         out_shape=(block, block, block, block, small, small),
-        in_specs=[vmem] * 3,
-        out_specs=(vmem,) * 6,
-        compiler_params=pltpu.CompilerParams(vmem_limit_bytes=32 * 2**20),
+        in_specs=[hbm] * 2,
+        out_specs=(hbm,) * 4 + (vmem,) * 2,
+        scratch_shapes=[
+            pltpu.VMEM((2, RANK, 896), F32),
+            pltpu.VMEM((2, OWN, C), F32),
+            pltpu.VMEM((2, OWN, C), F32),
+            pltpu.VMEM((2, OWN, C), F32),
+            pltpu.SemaphoreType.DMA((7,)),
+        ],
+        compiler_params=pltpu.CompilerParams(vmem_limit_bytes=60 * 2**20),
         name="finish",
-    )(merged, left, right)
+    )(merged, table)
     return approx_one, approx_two, fresh_one[None], fresh_two[None], new_one.T, new_two.T
 
 

time: 69.5 us -> 59.3 us (0.85); the launches traced: 68.4 us -> 58.9 us
  Pallas kernels: 65.1 us -> 58.3 us
  local copies, waits for them, and re-layouts: 2.65 us -> 0 us
    pallas_call x1, Pallas kernels: 62.3 us -> 53.4 us  [on_device(): pl.pallas_call(train_kernel, out_shape=(sds((2, OWN, C), F32), sds((2, RA...]
    unnamed x6 -> x0, local copies, waits for them, and re-layouts: 2.65 us -> none
    pallas_call x1, Pallas kernels: 2.82 us -> 4.87 us  [on_device(): pl.pallas_call(finish_kernel, out_shape=(block, block, block, block, smal...]
where the time goes in v2:
time: 59.3 us; the launch traced here: 58.9 us
  Pallas kernels  58.3 us (98%)
  between operations  0.64 us (1%)
    pallas_call x1, Pallas kernels, on_device(): pl.pallas_call(train_kernel, out_shape=(sds((2, OWN, C), F32), sds((2, RA...  53.4 us
    pallas_call x1, Pallas kernels, on_device(): pl.pallas_call(finish_kernel, out_shape=(block, block, block, block, smal...  4.87 us

profile of v2, /device:TPU:1, one launch (start us, length us, event | category | flops | bytes accessed | tf_op | source)
XLA Modules:
  0.0 58.9 jit_solution(13098788145869745987)
XLA Ops:
  0.6 53.4 %train.1 = (f32[2,432,256]{2,1,0:T(8,128)}, f32[2,8,896]{2,1,0:T(8,128)}) custom-call(bf16[5,64,256]{2,1,0:T(8,128)(2,1)} %bitcast.12, bf16[5,64,256]{2,1,0:T(8,128)(2,1)} %bitcast.13, bf16[6912,256]{1,0:T(8,128)(2,1)} %ker_one.1, bf16[6912,256]{1,0:T(8,128)(2,1)} %ker_two.1, f32[432,256]{1,0:T(8,128)} %bitcast.10, f32[432,256]{1,0:T(8,128)} %bitcast.11, ...), custom_call_target="tpu_custom_call" | custom-call | tf_op jit(solution)/shard_map/train/pallas_call | solution.py:542
  54.1 4.9 %finish.1 = (f32[432,256]{1,0:T(8,128)}, f32[432,256]{1,0:T(8,128)}, f32[432,256]{1,0:T(8,128)}, f32[432,256]{1,0:T(8,128)}, f32[8,256]{1,0:T(8,128)}, /*index=5*/f32[8,256]{1,0:T(8,128)}) custom-call(f32[2,432,256]{2,1,0:T(8,128)} %get-tuple-element.14.merged, f32[2,8,896]{2,1,0:T(8,128)} %get-tuple-element.15.table_in), custom_call_target="tpu_custom_call" | custom-call | tf_op jit(solution)/shard_map/finish/pallas_call | solution.py:602

commit v3 on v2

--- a/solution.py
+++ b/solution.py
@@ -129,32 +129,36 @@
     up, down = lax.rem(tile + 15, 16), lax.rem(tile + 1, 16)
 
     region = pl.when(tile >= 0)
-    sends = []
-    n_send = [0]
-
-    def remote(src, dst, recv, device):
-        copy = pltpu.make_async_remote_copy(
-            src_ref=src, dst_ref=dst, send_sem=send_sem.at[n_send[0]], recv_sem=recv_sem.at[recv],
+    totals = {}
+
+    def remote(src, dst, phase, device, total=None):
+        if phase not in totals:
+            totals[phase] = dst if total is None else total
+        pltpu.make_async_remote_copy(
+            src_ref=src, dst_ref=dst, send_sem=send_sem.at[phase], recv_sem=recv_sem.at[phase],
             device_id=device, device_id_type=MESH,
+        ).start()
+
+    def whole(phase):
+        ref = totals[phase]
+        return pltpu.make_async_remote_copy(
+            src_ref=ref, dst_ref=ref, send_sem=send_sem.at[phase], recv_sem=recv_sem.at[phase],
+            device_id={"tile": up}, device_id_type=MESH,
         )
-        n_send[0] += 1
-        copy.start()
-        sends.append(copy)
-
-    def arrived(dst, recv):
-        pltpu.make_async_remote_copy(
-            src_ref=dst, dst_ref=dst, send_sem=send_sem.at[0], recv_sem=recv_sem.at[recv],
-            device_id={"tile": up}, device_id_type=MESH,
-        ).wait_recv()
+
+    def arrived(phase):
+        whole(phase).wait_recv()
 
     def send_block(k, d):
         to = {"tile": along("y" if k else "z", d)}
-        remote(slopes.at[k, :, 0], slopes.at[k, :, d], 16 - 4 * k + d, to)
+        for f in range(FR):
+            remote(slopes.at[k, f, 0], slopes.at[k, f, d], 8 + k, to, slopes.at[k, :, pl.ds(1, 3)])
 
     def send_part(k, a, d):
         to = {"tile": along("z" if k else "y", d)}
         target = lax.rem((tz if k else ty) + d, 4)
-        remote(part_half.at[k, a, target], part_in.at[k, d, a], 92 + 9 * k + 3 * a + d - 1, to)
+        total = part_in.at[k, pl.ds(1, 3)]
+        remote(part_half.at[k, a, target], part_in.at[k, d, a], 10 + k, to, total)
 
     def send_slopes(k):
         factor = split((fac_two if k else fac_one)[...])
@@ -163,13 +167,13 @@
         thin[k, 0] = out[0:8] + out[8:16] + out[16:24]
         axis = "y" if k else "z"
         for d in range(1, 4):
-            remote(thin.at[k, 0], thin.at[k, d], 28 + 4 * k + d, {"tile": along(axis, d)})
+            to = {"tile": along(axis, d)}
+            remote(thin.at[k, 0], thin.at[k, d], 6 + k, to, thin.at[k, pl.ds(1, 3)])
         for d in (1, 3, 2) if k else (1, 3):
             send_block(k, d)
 
     def gradients(k):
-        for d in range(1, 4):
-            arrived(slopes.at[k, :, d], 16 - 4 * k + d)
+        arrived(8 + k)
         mine = tz if k else ty
 
         @region
@@ -185,6 +189,34 @@
                 half = out.astype(BF)
                 part_half[k, a] = half
                 part_rest[k, a] = (out - half.astype(F32)).astype(BF)
+
+    def project_errors():
+        for k in range(2):
+            mine = tz if k else ty
+            for half in range(2):
+                loads[4 + 2 * k + half].wait()
+
+            @region
+            def _(k=k, mine=mine):
+                for half in range(2):
+                    for tap in range(27):
+                        rows = errs[k, half, pl.ds(tap, 16, stride=27), :]
+                        err_rows[k, tap // 9, pl.ds((tap % 9) * 16, 16), pl.ds(half * 128, 128)] = rows
+                out = err_rows[k].reshape(OWN, C)
+                high = out.astype(BF)
+                rest = (out - high.astype(F32)).astype(BF)
+                factor = split((fac_two if k else fac_one)[...])
+                out = lax.dot_general(factor, high, NT, preferred_element_type=F32)
+                out += lax.dot_general(factor, rest, NT, preferred_element_type=F32)
+                out = out[0:8] + out[8:16] + out[16:24]
+                err_proj[k] = jnp.concatenate(
+                    [
+                        jnp.where(mine == j, out[:, a * 144 : a * 144 + 144], 0.0)
+                        for a in range(3)
+                        for j in range(4)
+                    ],
+                    axis=1,
+                )
 
     loads = [
         pltpu.make_async_copy(ker_one, raw.at[0], local_sem.at[0]),
@@ -208,13 +240,6 @@
     greeted += [pair] + [member(dx, dg) for dx, dg in group if dx]
     for device in greeted:
         pl.semaphore_signal(barrier, inc=1, device_id=device, device_id_type=MESH)
-    pl.semaphore_wait(barrier, len(greeted))
-
-    remote(lat.at[:, pl.ds(32, 32)], lat_ext.at[:, pl.ds(0, 32)], 0, {"tile": down})
-    remote(lat.at[:, pl.ds(0, 32)], lat_ext.at[:, pl.ds(96, 32)], 1, {"tile": up})
-    remote(cot.at[:, pl.ds(48, 16)], cot_ext.at[:, pl.ds(0, 16)], 2, {"tile": down})
-    remote(cot.at[:, pl.ds(0, 16)], cot_ext.at[:, pl.ds(80, 16)], 3, {"tile": up})
-
     held = lax.broadcasted_iota(jnp.int32, (256, 128), 0)
     want = lax.broadcasted_iota(jnp.int32, (256, 128), 1)
     same = (held // 128) == (want // 64)
@@ -228,6 +253,13 @@
     source = lax.broadcasted_iota(jnp.int32, (OWN, OWN), 0)
     target = lax.broadcasted_iota(jnp.int32, (OWN, OWN), 1)
     order[...] = jnp.where(target == (source % 16) * 27 + source // 16, 1.0, 0.0).astype(BF)
+
+    pl.semaphore_wait(barrier, len(greeted))
+
+    remote(lat.at[:, pl.ds(32, 32)], lat_ext.at[:, pl.ds(0, 32)], 0, {"tile": down})
+    remote(lat.at[:, pl.ds(0, 32)], lat_ext.at[:, pl.ds(96, 32)], 1, {"tile": up})
+    remote(cot.at[:, pl.ds(48, 16)], cot_ext.at[:, pl.ds(0, 16)], 2, {"tile": down})
+    remote(cot.at[:, pl.ds(0, 16)], cot_ext.at[:, pl.ds(80, 16)], 3, {"tile": up})
 
     for k in range(2):
         loads[k].wait()
@@ -245,37 +277,10 @@
 
         lax.fori_loop(0, 16, reorder, 0)
 
-    for k in range(2):
-        mine = tz if k else ty
-        for half in range(2):
-            loads[4 + 2 * k + half].wait()
-
-        @region
-        def _(k=k, mine=mine):
-            for half in range(2):
-                for tap in range(27):
-                    rows = errs[k, half, pl.ds(tap, 16, stride=27), :]
-                    err_rows[k, tap // 9, pl.ds((tap % 9) * 16, 16), pl.ds(half * 128, 128)] = rows
-            out = err_rows[k].reshape(OWN, C)
-            high = out.astype(BF)
-            rest = (out - high.astype(F32)).astype(BF)
-            factor = split((fac_two if k else fac_one)[...])
-            out = lax.dot_general(factor, high, NT, preferred_element_type=F32)
-            out += lax.dot_general(factor, rest, NT, preferred_element_type=F32)
-            out = out[0:8] + out[8:16] + out[16:24]
-            err_proj[k] = jnp.concatenate(
-                [
-                    jnp.where(mine == j, out[:, a * 144 : a * 144 + 144], 0.0)
-                    for a in range(3)
-                    for j in range(4)
-                ],
-                axis=1,
-            )
-
     loads[2].wait()
     loads[3].wait()
-    arrived(lat_ext.at[:, pl.ds(0, 32)], 0)
-    arrived(lat_ext.at[:, pl.ds(96, 32)], 1)
+    arrived(0)
+    arrived(1)
 
     def enter_one(f, carry):
         field = lat_ext[f].astype(F32).reshape(16, WC, C)[1:15]
@@ -292,26 +297,27 @@
     own[0].start()
     for d in range(1, 4):
         to = lax.rem(tz + d, 4)
-        remote(turn.at[0, :, to], turn_in.at[0, d], 4 + d, {"tile": along("z", d)})
+        remote(turn.at[0, :, to], turn_in.at[0, d], 4, {"tile": along("z", d)}, turn_in.at[0, pl.ds(1, 3)])
     region(lambda: conv(even, odd, 12, weights.at[0], acc_one, False))
 
+    totals[5] = turn_in.at[1, pl.ds(1, 3)]
     def enter_two(f, carry):
         pre = acc_one[f]
         hidden = (pre * sigmoid(pre)).astype(BF).astype(F32).reshape(12, WC, C)
         hidden = valid_rows(hidden, -2, tile)
         turn[1, f] = turned(hidden[1:11])
+        for d in range(1, 4):
+            to = lax.rem(ty + d, 4)
+            remote(turn.at[1, f, :, to], turn_in.at[1, d, f], 5, {"tile": along("y", d)})
         spread(hidden, f, even, odd)
         return carry
 
     lax.fori_loop(0, FR, enter_two, 0)
     own[1].start()
-    for d in range(1, 4):
-        to = lax.rem(ty + d, 4)
-        remote(turn.at[1, :, :, to], turn_in.at[1, d], 8 + d, {"tile": along("y", d)})
     region(lambda: conv(even, odd, 10, weights.at[1], acc_two, False))
 
-    arrived(cot_ext.at[:, pl.ds(0, 16)], 2)
-    arrived(cot_ext.at[:, pl.ds(80, 16)], 3)
+    arrived(2)
+    arrived(3)
 
     def enter_three(f, carry):
         cots = cot_ext[f].astype(F32)[8:88]
@@ -334,9 +340,10 @@
     send_slopes(0)
 
     for k in range(2):
+        if k == 1:
+            project_errors()
         own[k].wait()
-        for d in range(1, 4):
-            arrived(turn_in.at[k, d], 4 + 4 * k + d)
+        arrived(4 + k)
 
         @region
         def _(k=k):
@@ -353,8 +360,7 @@
                             patches[k, rows, pl.ds(f * 256 + p * 128, 128)] = block
 
     for k in (1, 0):
-        for d in range(1, 4):
-            arrived(thin.at[k, d], 28 + 4 * k + d)
+        arrived(6 + k)
 
         @region
         def _(k=k):
@@ -362,70 +368,71 @@
             wide = jnp.concatenate(
                 [blocks[d][:, f * 64 : f * 64 + 64] for f in range(FR) for d in range(4)], axis=1
             )
-            wide = split(wide)
-            outs = []
-            for a in range(3):
-                count = 3 + a
-                out = lax.dot_general(
-                    wide[:, (2 - a) * 256 :], patches[k, :, pl.ds(0, count * 256)], NT,
-                    preferred_element_type=F32,
-                )
-                outs.append(out[0:8] + out[8:16] + out[16:24])
-            sample = jnp.concatenate(outs, axis=1) + err_proj[k]
+            shifts = [
+                jnp.concatenate([wide[:, (2 - a) * 256 :], jnp.zeros((8, (2 - a) * 256), F32)], axis=1)
+                if a < 2
+                else wide
+                for a in range(3)
+            ]
+            wide = split(jnp.concatenate(shifts, axis=0))
+            out = lax.dot_general(wide, patches[k], NT, preferred_element_type=F32)
+            out = out[0:24] + out[24:48] + out[48:72]
+            out = jnp.concatenate([out[0:8], out[8:16], out[16:24]], axis=1)
+            sample = out + err_proj[k]
             sample = jnp.concatenate([sample, jnp.zeros((8, 2048 - 1728), F32)], axis=1)
             for q in range(16):
                 proj[k, q] = sample[:, q * 128 : q * 128 + 128]
 
-    remote(proj.at[1 - core], proj_in, 36, pair)
-    arrived(proj_in, 36)
+    remote(proj.at[1 - core], proj_in, 12, pair)
+    arrived(12)
     for q in range(16):
         proj_in[q] = proj_in[q] + proj[core, q]
     for dx, dg in group:
         to = place(dx, dg)
-        remote(proj_in.at[to], left_in.at[here], 37 + here, member(dx, dg))
+        remote(proj_in.at[to], left_in.at[here], 13, member(dx, dg), left_in.at[pl.ds(0, 15)])
     left_in[here] = proj_in[here]
     send_block(0, 2)
 
-    gradients(1)
-    for dx, dg in group:
-        source = place(dx, dg)
-        arrived(left_in.at[source], 37 + source)
+    arrived(13)
     piece = left_in[0]
     for q in range(1, 16):
         piece = piece + left_in[q]
     lefts[core, here] = piece * 0.125
     for dx, dg in group:
-        remote(lefts.at[core, here], lefts.at[core, here], 53 + here, member(dx, dg))
+        block = lefts.at[core, here]
+        remote(block, block, 14, member(dx, dg), lefts.at[0, pl.ds(0, 15)])
+    gradients(1)
     for a in range(3):
         for d in (1, 3):
             send_part(1, a, d)
     gradients(0)
-    for d in (1, 3):
-        send_part(0, 2, d)
-    for dx, dg in group:
-        source = place(dx, dg)
-        arrived(lefts.at[core, source], 53 + source)
-    remote(lefts.at[core], lefts.at[core], 69, pair)
-    arrived(lefts.at[1 - core], 69)
+    for a in (2, 1):
+        for d in (1, 3):
+            send_part(0, a, d)
+    arrived(14)
+    remote(lefts.at[core], lefts.at[core], 15, pair)
+    arrived(15)
 
     for k in range(2):
 
         @region
         def _(k=k):
-            whole = jnp.concatenate([lefts[k, q] for q in range(16)], axis=1)[:, 0:1728]
-            pieces = split(whole)
+            rows_all = jnp.concatenate([lefts[k, q] for q in range(16)], axis=1)[:, 0:1728]
+            pieces = split(rows_all)
             out = jnp.dot(pieces, part_half[k].reshape(1728, C), preferred_element_type=F32)
             out += jnp.dot(pieces, part_rest[k].reshape(1728, C), preferred_element_type=F32)
             right[k] = out[0:8] + out[8:16] + out[16:24]
 
-    remote(right.at[1 - core], right_pair, 70, pair)
-    arrived(right_pair, 70)
+    remote(right.at[1 - core], right_pair, 16, pair)
+    arrived(16)
     right_in[here] = right_pair[...] + right[core]
     for dx, dg in group:
-        remote(right_in.at[here], right_in.at[here], 71 + here, member(dx, dg))
+        block = right_in.at[here]
+        remote(block, block, 17, member(dx, dg), right_in.at[pl.ds(0, 15)])
+    for d in (1, 3):
+        send_part(0, 0, d)
+    send_part(0, 2, 2)
     for a in range(2):
-        for d in (1, 3):
-            send_part(0, a, d)
         send_part(1, a, 2)
 
     for k in range(2):
@@ -433,48 +440,40 @@
 
         @region
         def _(k=k, mine=mine):
-            whole = jnp.concatenate([lefts[k, q] for q in range(16)], axis=1)[:, 0:1728]
-            gram = lax.dot_general(whole, whole, NT, precision=HIGH, preferred_element_type=F32)
+            rows_all = jnp.concatenate([lefts[k, q] for q in range(16)], axis=1)[:, 0:1728]
+            gram = lax.dot_general(rows_all, rows_all, NT, precision=HIGH, preferred_element_type=F32)
             grams[k] = jnp.concatenate([gram, jnp.zeros((8, 120), F32)], axis=1)
             rows = []
             for a in range(3):
                 found = jnp.zeros((8, 144), F32)
                 for j in range(4):
                     at = a * 576 + j * 144
-                    found = jnp.where(mine == j, whole[:, at : at + 144], found)
+                    found = jnp.where(mine == j, rows_all[:, at : at + 144], found)
                 rows.append(found)
             out = split(jnp.concatenate(rows, axis=1))
             out = jnp.dot(out, order[...], preferred_element_type=F32)
             table[k, :, pl.ds(0, OWN)] = out[0:8] + out[8:16] + out[16:24]
 
-    for dx, dg in group:
-        source = place(dx, dg)
-        arrived(right_in.at[source], 71 + source)
+    arrived(17)
     total = right_in[0]
     for q in range(1, 16):
         total = total + right_in[q]
     right_far[other, :, pl.ds(0, 256)] = total
     right_far[other, :, pl.ds(256, 128)] = grams[core]
     for d in range(1, 4):
-        remote(right_far.at[other], right_far.at[other], 87 + other, across(d))
+        block = right_far.at[other]
+        remote(block, block, 18, across(d), right_far.at[pl.ds(0, 3)])
     send_part(1, 2, 2)
-    for a in range(3):
+    for a in range(2):
         send_part(0, a, 2)
 
-    for d in range(1, 4):
-        source = lax.rem(other + d, 4)
-        arrived(right_far.at[source], 87 + source)
+    arrived(18)
     right_all[core] = right_far[0] + right_far[1] + right_far[2] + right_far[3]
-    remote(right_all.at[core], right_all.at[core], 91, pair)
-    arrived(right_all.at[1 - core], 91)
-    table[:, :, pl.ds(512, 384)] = right_all[...]
-
+    remote(right_all.at[core], right_all.at[core], 19, pair)
     stores = []
     for k in (1, 0):
         mine = tz if k else ty
-        for a in range(3):
-            for d in range(1, 4):
-                arrived(part_in.at[k, d, a], 92 + 9 * k + 3 * a + d - 1)
+        arrived(10 + k)
 
         @region
         def _(k=k, mine=mine):
@@ -490,10 +489,13 @@
 
         stores.append(pltpu.make_async_copy(whole_rows.at[k], merged.at[k], local_sem.at[k]))
         stores[-1].start()
+    arrived(19)
+    table[:, :, pl.ds(512, 384)] = right_all[...]
+
     for store in stores:
         store.wait()
-    for copy in sends:
-        copy.wait_send()
+    for phase in totals:
+        whole(phase).wait_send()
 
 
 def finish_kernel(
@@ -520,7 +522,10 @@
     ):
         basis = table[k, :, 0:OWN]
         factor = table[k, :, 512 : 512 + C] * 0.125
-        approx = lax.dot_general(basis, factor, TN, precision=HIGH, preferred_element_type=F32)
+        b, f = split(basis).astype(F32), split(factor)
+        b = jnp.concatenate([b[0:8], b[0:8], b[0:8], b[8:16], b[8:16], b[16:24]], axis=0)
+        f = jnp.concatenate([f[0:24].astype(F32), f[0:16].astype(F32), f[0:8].astype(F32)], axis=0)
+        approx = lax.dot_general(b.astype(BF), f.astype(BF), TN, preferred_element_type=F32)
         new_ref[...] = factor
         approx_ref[k] = approx
         stores.append(pltpu.make_async_copy(approx_ref.at[k], approx_out, sem.at[3 + k]))
@@ -581,8 +586,8 @@
             pltpu.VMEM((2, 8, 384), F32),
             pltpu.VMEM((2, OWN, C), F32),
             pltpu.SemaphoreType.DMA((12,)),
-            pltpu.SemaphoreType.DMA((96,)),
-            pltpu.SemaphoreType.DMA((110,)),
+            pltpu.SemaphoreType.DMA((20,)),
+            pltpu.SemaphoreType.DMA((20,)),
         ],
         compiler_params=pltpu.CompilerParams(
             collective_id=0, has_side_effects=True, vmem_limit_bytes=60 * 2**20

time: 59.3 us -> 54.8 us (0.924)
  Pallas kernels: 58.3 us -> 53.9 us
    pallas_call x1, Pallas kernels: 53.4 us -> 50.1 us  [on_device(): pl.pallas_call(train_kernel, out_shape=(sds((2, OWN, C), F32), sds((2, RA...]
    pallas_call x1, Pallas kernels: 4.87 us -> 3.84 us  [on_device(): pl.pallas_call(finish_kernel, out_shape=(block, block, block, block, smal...]
where the time goes in v3:
time: 54.8 us; the launch traced here: 54.6 us
  Pallas kernels  53.9 us (98%)
  between operations  0.64 us (1%)
    pallas_call x1, Pallas kernels, on_device(): pl.pallas_call(train_kernel, out_shape=(sds((2, OWN, C), F32), sds((2, RA...  50.1 us
    pallas_call x1, Pallas kernels, on_device(): pl.pallas_call(finish_kernel, out_shape=(block, block, block, block, smal...  3.84 us

profile of v3, /device:TPU:1, one launch (start us, length us, event | category | flops | bytes accessed | tf_op | source)
XLA Modules:
  0.0 54.6 jit_solution(7540917926220380654)
XLA Ops:
  0.6 50.1 %train.1 = (f32[2,432,256]{2,1,0:T(8,128)}, f32[2,8,896]{2,1,0:T(8,128)}) custom-call(bf16[5,64,256]{2,1,0:T(8,128)(2,1)} %bitcast.12, bf16[5,64,256]{2,1,0:T(8,128)(2,1)} %bitcast.13, bf16[6912,256]{1,0:T(8,128)(2,1)} %ker_one.1, bf16[6912,256]{1,0:T(8,128)(2,1)} %ker_two.1, f32[432,256]{1,0:T(8,128)} %bitcast.10, f32[432,256]{1,0:T(8,128)} %bitcast.11, ...), custom_call_target="tpu_custom_call" | custom-call | tf_op jit(solution)/shard_map/train/pallas_call | solution.py:547
  50.7 3.8 %finish.1 = (f32[432,256]{1,0:T(8,128)}, f32[432,256]{1,0:T(8,128)}, f32[432,256]{1,0:T(8,128)}, f32[432,256]{1,0:T(8,128)}, f32[8,256]{1,0:T(8,128)}, /*index=5*/f32[8,256]{1,0:T(8,128)}) custom-call(f32[2,432,256]{2,1,0:T(8,128)} %get-tuple-element.14.merged, f32[2,8,896]{2,1,0:T(8,128)} %get-tuple-element.15.table_in), custom_call_target="tpu_custom_call" | custom-call | tf_op jit(solution)/shard_map/finish/pallas_call | solution.py:607

commit v4 on v3

--- a/solution.py
+++ b/solution.py
@@ -96,8 +96,8 @@
     lat, cot, ker_one, ker_two, err_one, err_two, fac_one, fac_two,
     merged, table,
     raw, weights, chunk, lat_ext, cot_ext, even, odd, acc_one, acc_two, acc_three,
-    select, order, turn, turn_in, slopes, patches, part, part_half, part_rest, part_in, errs, err_rows,
-    err_proj, thin, proj, proj_in, left_in, lefts, right, grams, right_pair, right_in, right_far, right_all, whole_rows,
+    select, order, turn, turn_in, slopes, patches, part, part_half, part_rest, part_in, part_pass, part_sum, errs, err_rows,
+    err_proj, thin, proj, proj_in, left_in, lefts, right, right_in, right_tile, gram_in, right_all, whole_rows,
     local_sem, send_sem, recv_sem,
 ):
     tile = lax.axis_index("tile")
@@ -149,16 +149,48 @@
     def arrived(phase):
         whole(phase).wait_recv()
 
-    def send_block(k, d):
-        to = {"tile": along("y" if k else "z", d)}
+    def send_blocks(k):
         for f in range(FR):
-            remote(slopes.at[k, f, 0], slopes.at[k, f, d], 8 + k, to, slopes.at[k, :, pl.ds(1, 3)])
-
-    def send_part(k, a, d):
-        to = {"tile": along("z" if k else "y", d)}
-        target = lax.rem((tz if k else ty) + d, 4)
-        total = part_in.at[k, pl.ds(1, 3)]
-        remote(part_half.at[k, a, target], part_in.at[k, d, a], 10 + k, to, total)
+            for d in (1, 3):
+                to = {"tile": along("y" if k else "z", d)}
+                remote(slopes.at[k, f, 0], slopes.at[k, f, d], 8 + k, to, slopes.at[k, :, pl.ds(1, 2)])
+
+    def forward_blocks(k):
+        arrived(8 + k)
+        for f in range(FR):
+            for d, half in ((1, pl.ds(0, 32)), (3, pl.ds(32, 32))):
+                to = {"tile": along("y" if k else "z", d)}
+                remote(slopes.at[k, f, d, half], slopes.at[k, f, 2, half], 20 + k, to, slopes.at[k, :, 2])
+
+    low, high = pl.ds(0, 80), pl.ds(80, 64)
+
+    def send_far(k, a):
+        axis, mine = ("z", tz) if k else ("y", ty)
+        chunk_of = part_half.at[k, a, lax.rem(mine + 2, 4)]
+        remote(chunk_of.at[low], part_pass.at[k, a, low], 23 + k, {"tile": along(axis, 1)}, part_pass.at[k])
+        remote(chunk_of.at[high], part_pass.at[k, a, high], 23 + k, {"tile": along(axis, 3)})
+
+    def send_near(k, a):
+        axis, mine = ("z", tz) if k else ("y", ty)
+        after, before = part_half.at[k, a, lax.rem(mine + 1, 4)], part_half.at[k, a, lax.rem(mine + 3, 4)]
+        remote(after.at[high], part_in.at[k, 0, a, high], 10 + k, {"tile": along(axis, 1)}, part_in.at[k])
+        remote(before.at[low], part_in.at[k, 1, a, low], 10 + k, {"tile": along(axis, 3)})
+
+    def pass_on(k):
+        axis, mine = ("z", tz) if k else ("y", ty)
+        arrived(23 + k)
+
+        @region
+        def _():
+            for a in range(3):
+                for rows, step in ((low, 1), (high, 3)):
+                    own_part = part[k, a, lax.rem(mine + step, 4), rows, :]
+                    part_sum[k, a, rows, :] = (own_part + part_pass[k, a, rows, :].astype(F32)).astype(BF)
+
+        for a in range(3):
+            for rows, step in ((low, 1), (high, 3)):
+                to = {"tile": along(axis, step)}
+                remote(part_sum.at[k, a, rows], part_in.at[k, step // 2, a, rows], 10 + k, to)
 
     def send_slopes(k):
         factor = split((fac_two if k else fac_one)[...])
@@ -169,26 +201,28 @@
         for d in range(1, 4):
             to = {"tile": along(axis, d)}
             remote(thin.at[k, 0], thin.at[k, d], 6 + k, to, thin.at[k, pl.ds(1, 3)])
-        for d in (1, 3, 2) if k else (1, 3):
-            send_block(k, d)
+        send_blocks(k)
 
     def gradients(k):
-        arrived(8 + k)
+        arrived(20 + k)
         mine = tz if k else ty
-
-        @region
-        def _():
-            for a in range(3):
+        for a in range(3):
+
+            @region
+            def _(a=a):
                 count = 3 + a
                 rhs = slopes[k, pl.ds(2 - a, count)].reshape(count * 256, C)
                 out = jnp.dot(patches[k, :, pl.ds(0, count * 256)], rhs, preferred_element_type=F32)
                 part[k, a] = out.reshape(4, 144, C)
                 part[k, a, mine] += err_rows[k, a]
-            for a in range(3):
                 out = part[k, a]
                 half = out.astype(BF)
                 part_half[k, a] = half
                 part_rest[k, a] = (out - half.astype(F32)).astype(BF)
+
+            send_far(k, a)
+        for a in range(3):
+            send_near(k, a)
 
     def project_errors():
         for k in range(2):
@@ -234,10 +268,9 @@
         load.start()
 
     barrier = pltpu.get_barrier_semaphore()
-    greeted = [{"tile": up}, {"tile": down}]
-    greeted += [{"tile": along("y", d)} for d in range(1, 4)]
-    greeted += [{"tile": along("z", d)} for d in range(1, 4)]
+    greeted = [{"tile": lax.rem(tile + d, 16)} for d in range(1, 16)]
     greeted += [pair] + [member(dx, dg) for dx, dg in group if dx]
+    greeted += [{"rep": lax.rem(rx + d, 4) * 2 + 1 - core} for d in range(1, 4)]
     for device in greeted:
         pl.semaphore_signal(barrier, inc=1, device_id=device, device_id_type=MESH)
     held = lax.broadcasted_iota(jnp.int32, (256, 128), 0)
@@ -289,7 +322,7 @@
         spread(field, f, even, odd)
         return carry
 
-    lax.fori_loop(0, FR, enter_one, 0)
+    region(lambda: [enter_one(f, 0) for f in range(FR)] and None)
     own = [
         pltpu.make_async_copy(turn.at[0, :, tz], turn_in.at[0, 0], local_sem.at[6]),
         pltpu.make_async_copy(turn.at[1, :, :, ty], turn_in.at[1, 0], local_sem.at[7]),
@@ -306,13 +339,15 @@
         hidden = (pre * sigmoid(pre)).astype(BF).astype(F32).reshape(12, WC, C)
         hidden = valid_rows(hidden, -2, tile)
         turn[1, f] = turned(hidden[1:11])
-        for d in range(1, 4):
-            to = lax.rem(ty + d, 4)
-            remote(turn.at[1, f, :, to], turn_in.at[1, d, f], 5, {"tile": along("y", d)})
         spread(hidden, f, even, odd)
         return carry
 
-    lax.fori_loop(0, FR, enter_two, 0)
+    for group_of in ((0, 1), (2, 3, 4)):
+        region(lambda: [enter_two(f, 0) for f in group_of] and None)
+        for f in group_of:
+            for d in range(1, 4):
+                to = lax.rem(ty + d, 4)
+                remote(turn.at[1, f, :, to], turn_in.at[1, d, f], 5, {"tile": along("y", d)})
     own[1].start()
     region(lambda: conv(even, odd, 10, weights.at[1], acc_two, False))
 
@@ -327,7 +362,7 @@
         slopes[1, f, 0] = slope[1:9].reshape(64, C).astype(BF)
         return carry
 
-    lax.fori_loop(0, FR, enter_three, 0)
+    region(lambda: [enter_three(f, 0) for f in range(FR)] and None)
     send_slopes(1)
     region(lambda: conv(even, odd, 8, weights.at[1], acc_three, True))
 
@@ -336,7 +371,7 @@
         slopes[0, f, 0] = (acc_three[f] * silu_slope(pre)).astype(BF)
         return carry
 
-    lax.fori_loop(0, FR, leave, 0)
+    region(lambda: [leave(f, 0) for f in range(FR)] and None)
     send_slopes(0)
 
     for k in range(2):
@@ -391,7 +426,8 @@
         to = place(dx, dg)
         remote(proj_in.at[to], left_in.at[here], 13, member(dx, dg), left_in.at[pl.ds(0, 15)])
     left_in[here] = proj_in[here]
-    send_block(0, 2)
+    forward_blocks(1)
+    forward_blocks(0)
 
     arrived(13)
     piece = left_in[0]
@@ -402,13 +438,7 @@
         block = lefts.at[core, here]
         remote(block, block, 14, member(dx, dg), lefts.at[0, pl.ds(0, 15)])
     gradients(1)
-    for a in range(3):
-        for d in (1, 3):
-            send_part(1, a, d)
     gradients(0)
-    for a in (2, 1):
-        for d in (1, 3):
-            send_part(0, a, d)
     arrived(14)
     remote(lefts.at[core], lefts.at[core], 15, pair)
     arrived(15)
@@ -423,17 +453,12 @@
             out += jnp.dot(pieces, part_rest[k].reshape(1728, C), preferred_element_type=F32)
             right[k] = out[0:8] + out[8:16] + out[16:24]
 
-    remote(right.at[1 - core], right_pair, 16, pair)
-    arrived(16)
-    right_in[here] = right_pair[...] + right[core]
-    for dx, dg in group:
-        block = right_in.at[here]
-        remote(block, block, 17, member(dx, dg), right_in.at[pl.ds(0, 15)])
-    for d in (1, 3):
-        send_part(0, 0, d)
-    send_part(0, 2, 2)
-    for a in range(2):
-        send_part(1, a, 2)
+    for d in range(1, 4):
+        for on in (core, 1 - core):
+            to = {"rep": lax.rem(rx + d, 4) * 2 + on}
+            remote(right.at[on], right_in.at[rep], 17, to, right_in.at[pl.ds(0, 7)])
+    remote(right.at[1 - core], right_in.at[rep], 17, pair)
+    right_in[rep] = right[core]
 
     for k in range(2):
         mine = tz if k else ty
@@ -442,7 +467,12 @@
         def _(k=k, mine=mine):
             rows_all = jnp.concatenate([lefts[k, q] for q in range(16)], axis=1)[:, 0:1728]
             gram = lax.dot_general(rows_all, rows_all, NT, precision=HIGH, preferred_element_type=F32)
-            grams[k] = jnp.concatenate([gram, jnp.zeros((8, 120), F32)], axis=1)
+            gram = jnp.concatenate([gram, jnp.zeros((8, 120), F32)], axis=1)
+
+            @pl.when(core == k)
+            def _():
+                gram_in[other] = gram
+
             rows = []
             for a in range(3):
                 found = jnp.zeros((8, 144), F32)
@@ -454,21 +484,26 @@
             out = jnp.dot(out, order[...], preferred_element_type=F32)
             table[k, :, pl.ds(0, OWN)] = out[0:8] + out[8:16] + out[16:24]
 
+    for d in range(1, 4):
+        remote(gram_in.at[other], gram_in.at[other], 22, across(d), gram_in.at[pl.ds(0, 3)])
+
+    pass_on(1)
+    pass_on(0)
     arrived(17)
     total = right_in[0]
+    for q in range(1, 8):
+        total = total + right_in[q]
+    right_tile[tile] = total
+    for d in range(1, 16):
+        block = right_tile.at[tile]
+        remote(block, block, 18, {"tile": lax.rem(tile + d, 16)}, right_tile.at[pl.ds(0, 15)])
+    arrived(22)
+    right_all[core, :, pl.ds(256, 128)] = gram_in[0] + gram_in[1] + gram_in[2] + gram_in[3]
+    arrived(18)
+    total = right_tile[0]
     for q in range(1, 16):
-        total = total + right_in[q]
-    right_far[other, :, pl.ds(0, 256)] = total
-    right_far[other, :, pl.ds(256, 128)] = grams[core]
-    for d in range(1, 4):
-        block = right_far.at[other]
-        remote(block, block, 18, across(d), right_far.at[pl.ds(0, 3)])
-    send_part(1, 2, 2)
-    for a in range(2):
-        send_part(0, a, 2)
-
-    arrived(18)
-    right_all[core] = right_far[0] + right_far[1] + right_far[2] + right_far[3]
+        total = total + right_tile[q]
+    right_all[core, :, pl.ds(0, 256)] = total
     remote(right_all.at[core], right_all.at[core], 19, pair)
     stores = []
     for k in (1, 0):
@@ -480,7 +515,7 @@
             for tap in range(27):
                 a, rows = tap // 9, pl.ds((tap % 9) * 16, 16)
                 grad = part[k, a, mine, rows, :]
-                for d in range(1, 4):
+                for d in range(2):
                     grad = grad + part_in[k, d, a, rows, :].astype(F32)
                 for half in range(2):
                     chunk[half, pl.ds(tap, 16, stride=27), :] = grad[:, half * 128 : half * 128 + 128]
@@ -500,7 +535,7 @@
 
 def finish_kernel(
     merged, table_in, approx_one, approx_two, fresh_one, fresh_two, new_one, new_two,
-    table_ref, rows, approx_ref, fresh_ref, sem,
+    table_ref, rows, approx_ref, fresh_ref, factor_ref, sem,
 ):
     load = pltpu.make_async_copy(table_in, table_ref, sem.at[0])
     load.start()
@@ -517,7 +552,7 @@
         coefs = table[:, :, column : column + 1] * scale
         table = jnp.where(row == j, scaled, jnp.where(row > j, table - coefs * scaled, table))
     stores = []
-    for k, (approx_out, fresh_out, new_ref) in enumerate(
+    for k, (approx_out, fresh_out, new_out) in enumerate(
         ((approx_one, fresh_one, new_one), (approx_two, fresh_two, new_two))
     ):
         basis = table[k, :, 0:OWN]
@@ -526,7 +561,9 @@
         b = jnp.concatenate([b[0:8], b[0:8], b[0:8], b[8:16], b[8:16], b[16:24]], axis=0)
         f = jnp.concatenate([f[0:24].astype(F32), f[0:16].astype(F32), f[0:8].astype(F32)], axis=0)
         approx = lax.dot_general(b.astype(BF), f.astype(BF), TN, preferred_element_type=F32)
-        new_ref[...] = factor
+        factor_ref[k] = factor
+        stores.append(pltpu.make_async_copy(factor_ref.at[k], new_out, sem.at[7 + k]))
+        stores[-1].start()
         approx_ref[k] = approx
         stores.append(pltpu.make_async_copy(approx_ref.at[k], approx_out, sem.at[3 + k]))
         stores[-1].start()
@@ -569,7 +606,9 @@
             pltpu.VMEM((2, 3, 4, 144, C), F32),
             pltpu.VMEM((2, 3, 4, 144, C), BF),
             pltpu.VMEM((2, 3, 4, 144, C), BF),
-            pltpu.VMEM((2, 4, 3, 144, C), BF),
+            pltpu.VMEM((2, 2, 3, 144, C), BF),
+            pltpu.VMEM((2, 3, 144, C), BF),
+            pltpu.VMEM((2, 3, 144, C), BF),
             pltpu.VMEM((2, 2, OWN, 128), F32),
             pltpu.VMEM((2, 3, 144, C), F32),
             pltpu.VMEM((2, 8, 1728), F32),
@@ -579,15 +618,14 @@
             pltpu.VMEM((16, 8, 128), F32),
             pltpu.VMEM((2, 16, 8, 128), F32),
             pltpu.VMEM((2, 8, C), F32),
-            pltpu.VMEM((2, 8, 128), F32),
-            pltpu.VMEM((8, C), F32),
+            pltpu.VMEM((8, 8, C), F32),
             pltpu.VMEM((16, 8, C), F32),
-            pltpu.VMEM((4, 8, 384), F32),
+            pltpu.VMEM((4, 8, 128), F32),
             pltpu.VMEM((2, 8, 384), F32),
             pltpu.VMEM((2, OWN, C), F32),
             pltpu.SemaphoreType.DMA((12,)),
-            pltpu.SemaphoreType.DMA((20,)),
-            pltpu.SemaphoreType.DMA((20,)),
+            pltpu.SemaphoreType.DMA((25,)),
+            pltpu.SemaphoreType.DMA((25,)),
         ],
         compiler_params=pltpu.CompilerParams(
             collective_id=0, has_side_effects=True, vmem_limit_bytes=60 * 2**20
@@ -608,13 +646,14 @@
         finish_kernel,
         out_shape=(block, block, block, block, small, small),
         in_specs=[hbm] * 2,
-        out_specs=(hbm,) * 4 + (vmem,) * 2,
+        out_specs=(hbm,) * 6,
         scratch_shapes=[
             pltpu.VMEM((2, RANK, 896), F32),
             pltpu.VMEM((2, OWN, C), F32),
             pltpu.VMEM((2, OWN, C), F32),
             pltpu.VMEM((2, OWN, C), F32),
-            pltpu.SemaphoreType.DMA((7,)),
+            pltpu.VMEM((2, RANK, C), F32),
+            pltpu.SemaphoreType.DMA((9,)),
         ],
         compiler_params=pltpu.CompilerParams(vmem_limit_bytes=60 * 2**20),
         name="finish",

time: 54.8 us -> 51.8 us (0.945)
  Pallas kernels: 53.9 us -> 51 us
    pallas_call x1, Pallas kernels: 50.1 us -> 47.8 us  [on_device(): pl.pallas_call(train_kernel, out_shape=(sds((2, OWN, C), F32), sds((2, RA...]
    pallas_call x1, Pallas kernels: 3.84 us -> 3.25 us  [on_device(): pl.pallas_call(finish_kernel, out_shape=(block, block, block, block, smal...]
where the time goes in v4:
time: 51.8 us; the launch traced here: 51.7 us
  Pallas kernels  51 us (98%)
  between operations  0.64 us (1%)
    pallas_call x1, Pallas kernels, on_device(): pl.pallas_call(train_kernel, out_shape=(sds((2, OWN, C), F32), sds((2, RA...  47.8 us
    pallas_call x1, Pallas kernels, on_device(): pl.pallas_call(finish_kernel, out_shape=(block, block, block, block, smal...  3.25 us

profile of v4, /device:TPU:1, one launch (start us, length us, event | category | flops | bytes accessed | tf_op | source)
XLA Modules:
  0.0 51.7 jit_solution(9388439865664755889)
XLA Ops:
  0.6 47.8 %train.1 = (f32[2,432,256]{2,1,0:T(8,128)}, f32[2,8,896]{2,1,0:T(8,128)}) custom-call(bf16[5,64,256]{2,1,0:T(8,128)(2,1)} %bitcast.12, bf16[5,64,256]{2,1,0:T(8,128)(2,1)} %bitcast.13, bf16[6912,256]{1,0:T(8,128)(2,1)} %ker_one.1, bf16[6912,256]{1,0:T(8,128)(2,1)} %ker_two.1, f32[432,256]{1,0:T(8,128)} %bitcast.10, f32[432,256]{1,0:T(8,128)} %bitcast.11, ...), custom_call_target="tpu_custom_call" | custom-call | tf_op jit(solution)/shard_map/train/pallas_call | solution.py:584
  48.4 3.3 %finish.1 = (f32[432,256]{1,0:T(8,128)}, f32[432,256]{1,0:T(8,128)}, f32[432,256]{1,0:T(8,128)}, f32[432,256]{1,0:T(8,128)}, f32[8,256]{1,0:T(8,128)}, /*index=5*/f32[8,256]{1,0:T(8,128)}) custom-call(f32[2,432,256]{2,1,0:T(8,128)} %get-tuple-element.14.merged, f32[2,8,896]{2,1,0:T(8,128)} %get-tuple-element.15.table_in), custom_call_target="tpu_custom_call" | custom-call | tf_op jit(solution)/shard_map/finish/pallas_call | solution.py:645

commit v5 on v4

--- a/solution.py
+++ b/solution.py
@@ -94,10 +94,10 @@
 
 def train_kernel(
     lat, cot, ker_one, ker_two, err_one, err_two, fac_one, fac_two,
-    merged, table,
+    merged, table_out,
     raw, weights, chunk, lat_ext, cot_ext, even, odd, acc_one, acc_two, acc_three,
     select, order, turn, turn_in, slopes, patches, part, part_half, part_rest, part_in, part_pass, part_sum, errs, err_rows,
-    err_proj, thin, proj, proj_in, left_in, lefts, right, right_in, right_tile, gram_in, right_all, whole_rows,
+    err_proj, thin, proj, proj_in, left_in, lefts, right, right_in, right_tile, gram_in, gram_all, right_all, whole_rows, factors, table,
     local_sem, send_sem, recv_sem,
 ):
     tile = lax.axis_index("tile")
@@ -193,7 +193,7 @@
                 remote(part_sum.at[k, a, rows], part_in.at[k, step // 2, a, rows], 10 + k, to)
 
     def send_slopes(k):
-        factor = split((fac_two if k else fac_one)[...])
+        factor = split(factors[k])
         rows = slopes[k, :, 0].reshape(320, C)
         out = lax.dot_general(factor, rows, NT, preferred_element_type=F32)
         thin[k, 0] = out[0:8] + out[8:16] + out[16:24]
@@ -228,7 +228,7 @@
         for k in range(2):
             mine = tz if k else ty
             for half in range(2):
-                loads[4 + 2 * k + half].wait()
+                loads[6 + 2 * k + half].wait()
 
             @region
             def _(k=k, mine=mine):
@@ -239,7 +239,7 @@
                 out = err_rows[k].reshape(OWN, C)
                 high = out.astype(BF)
                 rest = (out - high.astype(F32)).astype(BF)
-                factor = split((fac_two if k else fac_one)[...])
+                factor = split(factors[k])
                 out = lax.dot_general(factor, high, NT, preferred_element_type=F32)
                 out += lax.dot_general(factor, rest, NT, preferred_element_type=F32)
                 out = out[0:8] + out[8:16] + out[16:24]
@@ -258,6 +258,8 @@
         pltpu.make_async_copy(lat, lat_ext.at[:, pl.ds(32, 64)], local_sem.at[2]),
         pltpu.make_async_copy(cot, cot_ext.at[:, pl.ds(16, 64)], local_sem.at[3]),
     ]
+    for k, fac in enumerate((fac_one, fac_two)):
+        loads.append(pltpu.make_async_copy(fac, factors.at[k], local_sem.at[4 + k]))
     for k, err in enumerate((err_one, err_two)):
         for half in range(2):
             lanes = pl.ds(half * 128, 128)
@@ -353,6 +355,8 @@
 
     arrived(2)
     arrived(3)
+    loads[4].wait()
+    loads[5].wait()
 
     def enter_three(f, carry):
         cots = cot_ext[f].astype(F32)[8:88]
@@ -482,7 +486,8 @@
                 rows.append(found)
             out = split(jnp.concatenate(rows, axis=1))
             out = jnp.dot(out, order[...], preferred_element_type=F32)
-            table[k, :, pl.ds(0, OWN)] = out[0:8] + out[8:16] + out[16:24]
+            out = out[0:8] + out[8:16] + out[16:24]
+            table[k, :, pl.ds(0, 512)] = jnp.concatenate([out, jnp.zeros((8, 80), F32)], axis=1)
 
     for d in range(1, 4):
         remote(gram_in.at[other], gram_in.at[other], 22, across(d), gram_in.at[pl.ds(0, 3)])
@@ -498,12 +503,29 @@
         block = right_tile.at[tile]
         remote(block, block, 18, {"tile": lax.rem(tile + d, 16)}, right_tile.at[pl.ds(0, 15)])
     arrived(22)
-    right_all[core, :, pl.ds(256, 128)] = gram_in[0] + gram_in[1] + gram_in[2] + gram_in[3]
+    gram_all[core] = gram_in[0] + gram_in[1] + gram_in[2] + gram_in[3]
+    remote(gram_all.at[core], gram_all.at[core], 16, pair)
+    arrived(16)
+
+    @region
+    def _():
+        row = lax.broadcasted_iota(jnp.int32, (2, RANK, 768), 1)
+        lane = lax.broadcasted_iota(jnp.int32, (2, RANK, 128), 2)
+        eye = jnp.where(lane == row[:, :, 0:128], 1.0, 0.0)
+        rows = jnp.concatenate([table[:, :, 0:512], gram_all[...], eye], axis=2)
+        for j in range(RANK):
+            scale = lax.rsqrt(rows[:, j : j + 1, 512 + j : 513 + j])
+            scaled = rows[:, j : j + 1, :] * scale
+            coefs = rows[:, :, 512 + j : 513 + j] * scale
+            rows = jnp.where(row == j, scaled, jnp.where(row > j, rows - coefs * scaled, rows))
+        table[:, :, pl.ds(0, 512)] = rows[:, :, 0:512]
+        table[:, :, pl.ds(768, 128)] = rows[:, :, 640:768]
+
     arrived(18)
     total = right_tile[0]
     for q in range(1, 16):
         total = total + right_tile[q]
-    right_all[core, :, pl.ds(0, 256)] = total
+    right_all[core] = total
     remote(right_all.at[core], right_all.at[core], 19, pair)
     stores = []
     for k in (1, 0):
@@ -525,7 +547,9 @@
         stores.append(pltpu.make_async_copy(whole_rows.at[k], merged.at[k], local_sem.at[k]))
         stores[-1].start()
     arrived(19)
-    table[:, :, pl.ds(512, 384)] = right_all[...]
+    table[:, :, pl.ds(512, C)] = right_all[...]
+    stores.append(pltpu.make_async_copy(table, table_out, local_sem.at[2]))
+    stores[-1].start()
 
     for store in stores:
         store.wait()
@@ -544,19 +568,16 @@
         copy.start()
     load.wait()
     table = table_ref[...]
-    row = lax.broadcasted_iota(jnp.int32, table.shape, 1)
-    for j in range(RANK):
-        column = 512 + C + j
-        scale = lax.rsqrt(table[:, j : j + 1, column : column + 1])
-        scaled = table[:, j : j + 1, :] * scale
-        coefs = table[:, :, column : column + 1] * scale
-        table = jnp.where(row == j, scaled, jnp.where(row > j, table - coefs * scaled, table))
+    factors = table[:, :, 768:769] * table[:, 0:1, 512:768]
+    for j in range(1, RANK):
+        factors += table[:, :, 768 + j : 769 + j] * table[:, j : j + 1, 512:768]
+    factors = factors * 0.125
     stores = []
     for k, (approx_out, fresh_out, new_out) in enumerate(
         ((approx_one, fresh_one, new_one), (approx_two, fresh_two, new_two))
     ):
         basis = table[k, :, 0:OWN]
-        factor = table[k, :, 512 : 512 + C] * 0.125
+        factor = factors[k]
         b, f = split(basis).astype(F32), split(factor)
         b = jnp.concatenate([b[0:8], b[0:8], b[0:8], b[8:16], b[8:16], b[16:24]], axis=0)
         f = jnp.concatenate([f[0:24].astype(F32), f[0:16].astype(F32), f[0:8].astype(F32)], axis=0)
@@ -584,8 +605,8 @@
     merged, table = pl.pallas_call(
         train_kernel,
         out_shape=(sds((2, OWN, C), F32), sds((2, RANK, 896), F32)),
-        in_specs=[hbm] * 6 + [vmem] * 2,
-        out_specs=(hbm, vmem),
+        in_specs=[hbm] * 8,
+        out_specs=(hbm, hbm),
         scratch_shapes=[
             pltpu.VMEM((2, 6912, C), BF),
             pltpu.VMEM((2, 3, 9 * C, C), BF),
@@ -621,8 +642,11 @@
             pltpu.VMEM((8, 8, C), F32),
             pltpu.VMEM((16, 8, C), F32),
             pltpu.VMEM((4, 8, 128), F32),
-            pltpu.VMEM((2, 8, 384), F32),
+            pltpu.VMEM((2, 8, 128), F32),
+            pltpu.VMEM((2, 8, C), F32),
             pltpu.VMEM((2, OWN, C), F32),
+            pltpu.VMEM((2, RANK, C), F32),
+            pltpu.VMEM((2, RANK, 896), F32),
             pltpu.SemaphoreType.DMA((12,)),
             pltpu.SemaphoreType.DMA((25,)),
             pltpu.SemaphoreType.DMA((25,)),

time: 51.8 us -> 50.4 us (0.973)
  Pallas kernels: 51 us -> 49.6 us
    pallas_call x1, Pallas kernels: 3.25 us -> 2.53 us  [on_device(): pl.pallas_call(finish_kernel, out_shape=(block, block, block, block, smal...]
    pallas_call x1, Pallas kernels: 47.8 us -> 47.1 us  [on_device(): pl.pallas_call(train_kernel, out_shape=(sds((2, OWN, C), F32), sds((2, RA...]
where the time goes in v5:
time: 50.4 us; the launch traced here: 50.3 us
  Pallas kernels  49.6 us (98%)
  between operations  0.64 us (1%)
    pallas_call x1, Pallas kernels, on_device(): pl.pallas_call(train_kernel, out_shape=(sds((2, OWN, C), F32), sds((2, RA...  47.1 us
    pallas_call x1, Pallas kernels, on_device(): pl.pallas_call(finish_kernel, out_shape=(block, block, block, block, smal...  2.53 us

profile of v5, /device:TPU:1, one launch (start us, length us, event | category | flops | bytes accessed | tf_op | source)
XLA Modules:
  0.0 50.3 jit_solution(5697650929733699334)
XLA Ops:
  0.6 47.1 %train.1 = (f32[2,432,256]{2,1,0:T(8,128)}, f32[2,8,896]{2,1,0:T(8,128)}) custom-call(bf16[5,64,256]{2,1,0:T(8,128)(2,1)} %bitcast.12, bf16[5,64,256]{2,1,0:T(8,128)(2,1)} %bitcast.13, bf16[6912,256]{1,0:T(8,128)(2,1)} %ker_one.1, bf16[6912,256]{1,0:T(8,128)(2,1)} %ker_two.1, f32[432,256]{1,0:T(8,128)} %bitcast.10, f32[432,256]{1,0:T(8,128)} %bitcast.11, ...), custom_call_target="tpu_custom_call" | custom-call | tf_op jit(solution)/shard_map/train/pallas_call | solution.py:605
  47.8 2.5 %finish.1 = (f32[432,256]{1,0:T(8,128)}, f32[432,256]{1,0:T(8,128)}, f32[432,256]{1,0:T(8,128)}, f32[432,256]{1,0:T(8,128)}, f32[8,256]{1,0:T(8,128)}, /*index=5*/f32[8,256]{1,0:T(8,128)}) custom-call(f32[2,432,256]{2,1,0:T(8,128)} %get-tuple-element.14.merged, f32[2,8,896]{2,1,0:T(8,128)} %get-tuple-element.15.table_in), custom_call_target="tpu_custom_call" | custom-call | tf_op jit(solution)/shard_map/finish/pallas_call | solution.py:669

commit v6 on v5

--- a/solution.py
+++ b/solution.py
@@ -78,10 +78,13 @@
             total[pl.ds(first_out, count)] += out
 
 
-def turned(field):
-    flat = field.reshape(80, C)
-    flat = jnp.concatenate([flat, jnp.zeros((48, C), F32)], axis=0)
-    return flat.T.astype(BF).reshape(4, 4, 16, 128)
+def row_tiles(v):
+    return v.reshape(FR, 8, WC, 2, 128).transpose(0, 1, 3, 2, 4).reshape(FR, 8, 16, 128)
+
+
+def rows_of(v):
+    v = v.astype(F32)
+    return jnp.concatenate([v[:, 0:8], v[:, 8:16]], axis=2)
 
 
 def split(v):
@@ -96,7 +99,7 @@
     lat, cot, ker_one, ker_two, err_one, err_two, fac_one, fac_two,
     merged, table_out,
     raw, weights, chunk, lat_ext, cot_ext, even, odd, acc_one, acc_two, acc_three,
-    select, order, turn, turn_in, slopes, patches, part, part_half, part_rest, part_in, part_pass, part_sum, errs, err_rows,
+    select, order, flat, turn, turn_in, slopes, patches, part, part_half, part_rest, part_in, part_pass, part_sum, errs, err_rows,
     err_proj, thin, proj, proj_in, left_in, lefts, right, right_in, right_tile, gram_in, gram_all, right_all, whole_rows, factors, table,
     local_sem, send_sem, recv_sem,
 ):
@@ -255,8 +258,8 @@
     loads = [
         pltpu.make_async_copy(ker_one, raw.at[0], local_sem.at[0]),
         pltpu.make_async_copy(ker_two, raw.at[1], local_sem.at[1]),
-        pltpu.make_async_copy(lat, lat_ext.at[:, pl.ds(32, 64)], local_sem.at[2]),
-        pltpu.make_async_copy(cot, cot_ext.at[:, pl.ds(16, 64)], local_sem.at[3]),
+        pltpu.make_async_copy(lat, lat_ext.at[:, pl.ds(3, 8)], local_sem.at[2]),
+        pltpu.make_async_copy(cot, cot_ext.at[:, pl.ds(1, 8)], local_sem.at[3]),
     ]
     for k, fac in enumerate((fac_one, fac_two)):
         loads.append(pltpu.make_async_copy(fac, factors.at[k], local_sem.at[4 + k]))
@@ -289,12 +292,15 @@
     target = lax.broadcasted_iota(jnp.int32, (OWN, OWN), 1)
     order[...] = jnp.where(target == (source % 16) * 27 + source // 16, 1.0, 0.0).astype(BF)
 
+    for k in range(2):
+        flat[k, pl.ds(400, 112), :] = jnp.zeros((112, C), F32)
+
     pl.semaphore_wait(barrier, len(greeted))
 
-    remote(lat.at[:, pl.ds(32, 32)], lat_ext.at[:, pl.ds(0, 32)], 0, {"tile": down})
-    remote(lat.at[:, pl.ds(0, 32)], lat_ext.at[:, pl.ds(96, 32)], 1, {"tile": up})
-    remote(cot.at[:, pl.ds(48, 16)], cot_ext.at[:, pl.ds(0, 16)], 2, {"tile": down})
-    remote(cot.at[:, pl.ds(0, 16)], cot_ext.at[:, pl.ds(80, 16)], 3, {"tile": up})
+    remote(lat.at[:, pl.ds(5, 3)], lat_ext.at[:, pl.ds(0, 3)], 0, {"tile": down})
+    remote(lat.at[:, pl.ds(0, 3)], lat_ext.at[:, pl.ds(11, 3)], 1, {"tile": up})
+    remote(cot.at[:, pl.ds(7, 1)], cot_ext.at[:, pl.ds(0, 1)], 2, {"tile": down})
+    remote(cot.at[:, pl.ds(0, 1)], cot_ext.at[:, pl.ds(9, 1)], 3, {"tile": up})
 
     for k in range(2):
         loads[k].wait()
@@ -318,13 +324,22 @@
     arrived(1)
 
     def enter_one(f, carry):
-        field = lat_ext[f].astype(F32).reshape(16, WC, C)[1:15]
+        field = rows_of(lat_ext[f])
         field = valid_rows(field, -3, tile)
-        turn[0, f] = turned(field[2:12])
+        flat[0, pl.ds(f * 80, 80), :] = field[2:12].reshape(80, C)
         spread(field, f, even, odd)
         return carry
 
-    region(lambda: [enter_one(f, 0) for f in range(FR)] and None)
+    def transpose(k, first, last):
+        for t in range(first, last):
+            turn[k, t] = flat[k, pl.ds(t * 128, 128), :].T.astype(BF).reshape(4, 4, 16, 128)
+
+    @region
+    def _():
+        for f in range(FR):
+            enter_one(f, 0)
+        transpose(0, 0, 4)
+
     own = [
         pltpu.make_async_copy(turn.at[0, :, tz], turn_in.at[0, 0], local_sem.at[6]),
         pltpu.make_async_copy(turn.at[1, :, :, ty], turn_in.at[1, 0], local_sem.at[7]),
@@ -340,16 +355,22 @@
         pre = acc_one[f]
         hidden = (pre * sigmoid(pre)).astype(BF).astype(F32).reshape(12, WC, C)
         hidden = valid_rows(hidden, -2, tile)
-        turn[1, f] = turned(hidden[1:11])
+        flat[1, pl.ds(f * 80, 80), :] = hidden[1:11].reshape(80, C)
         spread(hidden, f, even, odd)
         return carry
 
-    for group_of in ((0, 1), (2, 3, 4)):
-        region(lambda: [enter_two(f, 0) for f in group_of] and None)
-        for f in group_of:
+    for frames, first, last in (((0, 1), 0, 1), ((2, 3, 4), 1, 4)):
+
+        @region
+        def _():
+            for f in frames:
+                enter_two(f, 0)
+            transpose(1, first, last)
+
+        for t in range(first, last):
             for d in range(1, 4):
                 to = lax.rem(ty + d, 4)
-                remote(turn.at[1, f, :, to], turn_in.at[1, d, f], 5, {"tile": along("y", d)})
+                remote(turn.at[1, t, :, to], turn_in.at[1, d, t], 5, {"tile": along("y", d)})
     own[1].start()
     region(lambda: conv(even, odd, 10, weights.at[1], acc_two, False))
 
@@ -359,7 +380,7 @@
     loads[5].wait()
 
     def enter_three(f, carry):
-        cots = cot_ext[f].astype(F32)[8:88]
+        cots = rows_of(cot_ext[f]).reshape(80, C)
         slope = (cots * silu_slope(acc_two[f])).astype(BF).astype(F32).reshape(10, WC, C)
         slope = valid_rows(slope, -1, tile)
         spread(slope, f, even, odd)
@@ -387,9 +408,13 @@
         @region
         def _(k=k):
             for p in range(2):
-                lhs = jnp.concatenate(
-                    [turn_in[k, 2 * p + s].reshape(320, 128) for s in range(2)], axis=1
-                )
+                blocks = []
+                for s in range(2):
+                    wide = [turn_in[k, 2 * p + s, t].reshape(64, 128) for t in range(4)]
+                    wide = jnp.concatenate(wide, axis=1)
+                    wide = [wide[:, f * 80 : f * 80 + 128] for f in range(FR)]
+                    blocks.append(jnp.concatenate(wide, axis=0))
+                lhs = jnp.concatenate(blocks, axis=1)
                 out = jnp.dot(lhs, select[...], preferred_element_type=F32).astype(BF)
                 for f in range(FR):
                     for i in range(9):
@@ -611,8 +636,8 @@
             pltpu.VMEM((2, 6912, C), BF),
             pltpu.VMEM((2, 3, 9 * C, C), BF),
             pltpu.VMEM((2, OWN, 128), F32),
-            pltpu.VMEM((FR, 128, C), BF),
-            pltpu.VMEM((FR, 96, C), BF),
+            pltpu.VMEM((FR, 14, 16, 128), BF),
+            pltpu.VMEM((FR, 10, 16, 128), BF),
             pltpu.VMEM((3, FR, 112, C), BF),
             pltpu.VMEM((3, FR, 96, C), BF),
             pltpu.VMEM((FR, 96, C), F32),
@@ -620,8 +645,9 @@
             pltpu.VMEM((FR, 64, C), F32),
             pltpu.VMEM((256, 9 * 128), BF),
             pltpu.VMEM((OWN, OWN), BF),
-            pltpu.VMEM((2, FR, 4, 4, 16, 128), BF),
-            pltpu.VMEM((2, 4, FR, 4, 16, 128), BF),
+            pltpu.VMEM((2, 512, C), F32),
+            pltpu.VMEM((2, 4, 4, 4, 16, 128), BF),
+            pltpu.VMEM((2, 4, 4, 4, 16, 128), BF),
             pltpu.VMEM((2, FR, 4, 64, C), BF),
             pltpu.VMEM((2, 9 * 64, FR * 256), BF),
             pltpu.VMEM((2, 3, 4, 144, C), F32),
@@ -656,8 +682,8 @@
         ),
         name="train",
     )(
-        latents.reshape(FR, 64, C),
-        cotangent.reshape(FR, 64, C),
+        row_tiles(latents[0]),
+        row_tiles(cotangent[0]),
         kernel_one,
         kernel_two,
         error_one[0],

time: 50.4 us -> 49.6 us (0.984)
  Pallas kernels: 49.6 us -> 48.9 us
    pallas_call x1, Pallas kernels: 47.1 us -> 46.4 us  [on_device(): pl.pallas_call(train_kernel, out_shape=(sds((2, OWN, C), F32), sds((2, RA...]
where the time goes in v6:
time: 49.6 us; the launch traced here: 49.5 us
  Pallas kernels  48.9 us (99%)
  between operations  0.64 us (1%)
    pallas_call x1, Pallas kernels, on_device(): pl.pallas_call(train_kernel, out_shape=(sds((2, OWN, C), F32), sds((2, RA...  46.4 us
    pallas_call x1, Pallas kernels, on_device(): pl.pallas_call(finish_kernel, out_shape=(block, block, block, block, smal...  2.53 us

profile of v6, /device:TPU:1, one launch (start us, length us, event | category | flops | bytes accessed | tf_op | source)
XLA Modules:
  0.0 49.5 jit_solution(3349713720756383625)
XLA Ops:
  0.6 46.4 %train.1 = (f32[2,432,256]{2,1,0:T(8,128)}, f32[2,8,896]{2,1,0:T(8,128)}) custom-call(bf16[5,8,16,128]{3,2,1,0:T(8,128)(2,1)} %bitcast.20, bf16[5,8,16,128]{3,2,1,0:T(8,128)(2,1)} %bitcast.21, bf16[6912,256]{1,0:T(8,128)(2,1)} %ker_one.1, bf16[6912,256]{1,0:T(8,128)(2,1)} %ker_two.1, f32[432,256]{1,0:T(8,128)} %bitcast.18, f32[432,256]{1,0:T(8,128)} %bitcast.19, ...), custom_call_target="tpu_custom_call" | custom-call | tf_op jit(solution)/shard_map/train/pallas_call | solution.py:630
  47.0 2.5 %finish.1 = (f32[432,256]{1,0:T(8,128)}, f32[432,256]{1,0:T(8,128)}, f32[432,256]{1,0:T(8,128)}, f32[432,256]{1,0:T(8,128)}, f32[8,256]{1,0:T(8,128)}, /*index=5*/f32[8,256]{1,0:T(8,128)}) custom-call(f32[2,432,256]{2,1,0:T(8,128)} %get-tuple-element.14.merged, f32[2,8,896]{2,1,0:T(8,128)} %get-tuple-element.15.table_in), custom_call_target="tpu_custom_call" | custom-call | tf_op jit(solution)/shard_map/finish/pallas_call | solution.py:695

commit v7 on v6

--- a/solution.py
+++ b/solution.py
@@ -111,7 +111,10 @@
     other = core * ty + (1 - core) * tz
     here = rx * 4 + near
     pair = {"rep": rx * 2 + 1 - core}
-    group = [(dx, dg) for dx in range(4) for dg in range(4) if dx or dg]
+    group = sorted(
+        [(dx, dg) for dx in range(4) for dg in range(4) if dx or dg],
+        key=lambda step: -min(step[0], 4 - step[0]) - min(step[1], 4 - step[1]),
+    )
 
     def place(dx, dg):
         return lax.rem(rx + dx, 4) * 4 + lax.rem(near + dg, 4)
@@ -482,7 +485,7 @@
             out += jnp.dot(pieces, part_rest[k].reshape(1728, C), preferred_element_type=F32)
             right[k] = out[0:8] + out[8:16] + out[16:24]
 
-    for d in range(1, 4):
+    for d in (2, 1, 3):
         for on in (core, 1 - core):
             to = {"rep": lax.rem(rx + d, 4) * 2 + on}
             remote(right.at[on], right_in.at[rep], 17, to, right_in.at[pl.ds(0, 7)])
@@ -524,9 +527,10 @@
     for q in range(1, 8):
         total = total + right_in[q]
     right_tile[tile] = total
-    for d in range(1, 16):
+    for dz, dy in group:
         block = right_tile.at[tile]
-        remote(block, block, 18, {"tile": lax.rem(tile + d, 16)}, right_tile.at[pl.ds(0, 15)])
+        to = lax.rem(tz + dz, 4) * 4 + lax.rem(ty + dy, 4)
+        remote(block, block, 18, {"tile": to}, right_tile.at[pl.ds(0, 15)])
     arrived(22)
     gram_all[core] = gram_in[0] + gram_in[1] + gram_in[2] + gram_in[3]
     remote(gram_all.at[core], gram_all.at[core], 16, pair)

time: 49.6 us -> 49 us (0.988)
  Pallas kernels: 48.9 us -> 48.3 us
    pallas_call x1, Pallas kernels: 46.4 us -> 45.7 us  [on_device(): pl.pallas_call(train_kernel, out_shape=(sds((2, OWN, C), F32), sds((2, RA...]
where the time goes in v7:
time: 49 us; the launch traced here: 48.9 us
  Pallas kernels  48.3 us (99%)
  between operations  0.64 us (1%)
    pallas_call x1, Pallas kernels, on_device(): pl.pallas_call(train_kernel, out_shape=(sds((2, OWN, C), F32), sds((2, RA...  45.7 us
    pallas_call x1, Pallas kernels, on_device(): pl.pallas_call(finish_kernel, out_shape=(block, block, block, block, smal...  2.53 us

profile of v7, /device:TPU:1, one launch (start us, length us, event | category | flops | bytes accessed | tf_op | source)
XLA Modules:
  0.0 48.9 jit_solution(16505909144488131968)
XLA Ops:
  0.6 45.7 %train.1 = (f32[2,432,256]{2,1,0:T(8,128)}, f32[2,8,896]{2,1,0:T(8,128)}) custom-call(bf16[5,8,16,128]{3,2,1,0:T(8,128)(2,1)} %bitcast.20, bf16[5,8,16,128]{3,2,1,0:T(8,128)(2,1)} %bitcast.21, bf16[6912,256]{1,0:T(8,128)(2,1)} %ker_one.1, bf16[6912,256]{1,0:T(8,128)(2,1)} %ker_two.1, f32[432,256]{1,0:T(8,128)} %bitcast.18, f32[432,256]{1,0:T(8,128)} %bitcast.19, ...), custom_call_target="tpu_custom_call" | custom-call | tf_op jit(solution)/shard_map/train/pallas_call | solution.py:634
  46.4 2.5 %finish.1 = (f32[432,256]{1,0:T(8,128)}, f32[432,256]{1,0:T(8,128)}, f32[432,256]{1,0:T(8,128)}, f32[432,256]{1,0:T(8,128)}, f32[8,256]{1,0:T(8,128)}, /*index=5*/f32[8,256]{1,0:T(8,128)}) custom-call(f32[2,432,256]{2,1,0:T(8,128)} %get-tuple-element.14.merged, f32[2,8,896]{2,1,0:T(8,128)} %get-tuple-element.15.table_in), custom_call_target="tpu_custom_call" | custom-call | tf_op jit(solution)/shard_map/finish/pallas_call | solution.py:699

commit v8 on v7

--- a/solution.py
+++ b/solution.py
@@ -204,7 +204,7 @@
         out = lax.dot_general(factor, rows, NT, preferred_element_type=F32)
         thin[k, 0] = out[0:8] + out[8:16] + out[16:24]
         axis = "y" if k else "z"
-        for d in range(1, 4):
+        for d in (2, 1, 3):
             to = {"tile": along(axis, d)}
             remote(thin.at[k, 0], thin.at[k, d], 6 + k, to, thin.at[k, pl.ds(1, 3)])
         send_blocks(k)
@@ -276,7 +276,7 @@
         load.start()
 
     barrier = pltpu.get_barrier_semaphore()
-    greeted = [{"tile": lax.rem(tile + d, 16)} for d in range(1, 16)]
+    greeted = [{"tile": lax.rem(tz + dz, 4) * 4 + lax.rem(ty + dy, 4)} for dz, dy in group]
     greeted += [pair] + [member(dx, dg) for dx, dg in group if dx]
     greeted += [{"rep": lax.rem(rx + d, 4) * 2 + 1 - core} for d in range(1, 4)]
     for device in greeted:
@@ -348,7 +348,7 @@
         pltpu.make_async_copy(turn.at[1, :, :, ty], turn_in.at[1, 0], local_sem.at[7]),
     ]
     own[0].start()
-    for d in range(1, 4):
+    for d in (2, 1, 3):
         to = lax.rem(tz + d, 4)
         remote(turn.at[0, :, to], turn_in.at[0, d], 4, {"tile": along("z", d)}, turn_in.at[0, pl.ds(1, 3)])
     region(lambda: conv(even, odd, 12, weights.at[0], acc_one, False))
@@ -371,7 +371,7 @@
             transpose(1, first, last)
 
         for t in range(first, last):
-            for d in range(1, 4):
+            for d in (2, 1, 3):
                 to = lax.rem(ty + d, 4)
                 remote(turn.at[1, t, :, to], turn_in.at[1, d, t], 5, {"tile": along("y", d)})
     own[1].start()
@@ -517,7 +517,7 @@
             out = out[0:8] + out[8:16] + out[16:24]
             table[k, :, pl.ds(0, 512)] = jnp.concatenate([out, jnp.zeros((8, 80), F32)], axis=1)
 
-    for d in range(1, 4):
+    for d in (2, 1, 3):
         remote(gram_in.at[other], gram_in.at[other], 22, across(d), gram_in.at[pl.ds(0, 3)])
 
     pass_on(1)

time: 49 us -> 49 us (level)
  no operation moved by 1% of the time
where the time goes in v8:
time: 49 us; the launch traced here: 48.8 us
  Pallas kernels  48.2 us (98%)
  between operations  0.64 us (1%)
    pallas_call x1, Pallas kernels, on_device(): pl.pallas_call(train_kernel, out_shape=(sds((2, OWN, C), F32), sds((2, RA...  45.7 us
    pallas_call x1, Pallas kernels, on_device(): pl.pallas_call(finish_kernel, out_shape=(block, block, block, block, smal...  2.53 us

profile of v8, /device:TPU:1, one launch (start us, length us, event | category | flops | bytes accessed | tf_op | source)
XLA Modules:
  0.0 48.8 jit_solution(18147927944585613587)
XLA Ops:
  0.6 45.7 %train.1 = (f32[2,432,256]{2,1,0:T(8,128)}, f32[2,8,896]{2,1,0:T(8,128)}) custom-call(bf16[5,8,16,128]{3,2,1,0:T(8,128)(2,1)} %bitcast.20, bf16[5,8,16,128]{3,2,1,0:T(8,128)(2,1)} %bitcast.21, bf16[6912,256]{1,0:T(8,128)(2,1)} %ker_one.1, bf16[6912,256]{1,0:T(8,128)(2,1)} %ker_two.1, f32[432,256]{1,0:T(8,128)} %bitcast.18, f32[432,256]{1,0:T(8,128)} %bitcast.19, ...), custom_call_target="tpu_custom_call" | custom-call | tf_op jit(solution)/shard_map/train/pallas_call | solution.py:634
  46.3 2.5 %finish.1 = (f32[432,256]{1,0:T(8,128)}, f32[432,256]{1,0:T(8,128)}, f32[432,256]{1,0:T(8,128)}, f32[432,256]{1,0:T(8,128)}, f32[8,256]{1,0:T(8,128)}, /*index=5*/f32[8,256]{1,0:T(8,128)}) custom-call(f32[2,432,256]{2,1,0:T(8,128)} %get-tuple-element.14.merged, f32[2,8,896]{2,1,0:T(8,128)} %get-tuple-element.15.table_in), custom_call_target="tpu_custom_call" | custom-call | tf_op jit(solution)/shard_map/finish/pallas_call | solution.py:699
